TPU v7x, 32 devices: a whole 2x2x4 slice. The times are simulated.
32 devices in a mesh: groups: 2 (over x), wide: 8 (over z, y), narrow: 2 (over core).
Axes of the slice: x: 2, y: 2, z: 4, core: 2. Of those that a mesh axis runs over, the one named last changes fastest.
Arguments:
- plume_state: bfloat16 [64, 32, 128, 128], P('groups', 'wide', 'narrow'), parts along dimension 0, may hold values from -6 to 6
- spectral_weight: bfloat16 [2, 288, 24, 32, 64], P('narrow', 'wide'), may hold values from -0.75 to 0.75
- channel_mixer: bfloat16 [32, 32], replicated, may hold values from -1 to 1
- channel_bias: float32 [32], replicated, may hold values from -3 to 3
- upstream_grad: bfloat16 [64, 32, 128, 128], P('groups', 'wide', 'narrow'), parts along dimension 0, may hold values from -6 to 6
Outputs:
- layer_out: bfloat16 [64, 32, 128, 128], P('groups', 'wide', 'narrow'), parts along dimension 0
- state_grad: bfloat16 [64, 32, 128, 128], P('groups', 'wide', 'narrow'), parts along dimension 0
- weight_grad: float32 [2, 288, 48, 32, 64], P('narrow', 'wide', 'groups'), parts along dimension 2
There are 2 independent parts, one for each index of `groups`. A program takes and returns all parts, laid end to end along the dimension named above; an argument that names none is the same for every part. Nothing has to cross between parts.
All inputs are finite; a program needn't handle non-finite values.
Results may differ from a plain program's by a relative error of at most 0.015.
Values may be sent and summed in bfloat16 or wider, within the bound.
A program may use at most 128 MiB of HBM per device.

v0:
```python
import functools
import math

import jax
import jax.numpy as jnp
import numpy as np
from jax import lax
from jax.experimental import pallas as pl
from jax.experimental.pallas import tpu as pltpu
from jax.sharding import PartitionSpec as P

C = 32
MX = 24
MY = 24
MZ = 24
OCT = 8
F32 = jnp.float32
BF16 = jnp.bfloat16
VMEM_LIMIT = 50 * 1024 * 1024


def mm(left, right):
    return jnp.dot(left, right, preferred_element_type=F32)


def mm_nt(left, right):
    return lax.dot_general(left, right, (((1,), (1,)), ((), ())), preferred_element_type=F32)


def const(array):
    return jnp.asarray(np.asarray(array, np.float32)).astype(BF16)


def phases(points, frequency):
    turns = np.mod(frequency[:, None] * np.arange(points)[None, :], points)
    return turns.astype(np.float64) * (2.0 * math.pi / points)


def wave(points, modes, sign, scale):
    index = np.arange(modes)
    angles = phases(points, np.where(index < modes // 2, index, index - modes))
    return np.cos(angles) * scale, sign * np.sin(angles) * scale


def y_forward_table(points, parts, cells_x, scale):
    real, imag = wave(points, MY, -1.0, scale)
    local = np.stack([real, imag]).reshape(2, MY, parts, points // parts)
    table = np.einsum("sqnb,ac->nsaqcb", local, np.eye(cells_x))
    return const(table.reshape(parts, 2 * cells_x * MY, -1))


def y_inverse_table(points, parts, cells_x, scale):
    real, imag = wave(points, MY, 1.0, scale)
    local = np.stack([real, -imag]).reshape(2, MY, parts, points // parts)
    table = np.einsum("sqnb,ac->ncbsaq", local, np.eye(cells_x))
    return const(table.reshape(parts, -1, 2 * cells_x * MY))


def z_parts(points, first, other):
    angles = phases(points, np.arange(MZ))
    weight = np.where(np.arange(MZ) == 0, first, other)[:, None]
    return np.cos(angles) * weight, np.sin(angles) * weight


def z_forward_table(points, first, other):
    cos, sin = z_parts(points, first, other)
    table = np.zeros((2 * points, 128))
    table[:points, :MZ] = cos.T
    table[points:, :MZ] = sin.T
    table[:points, MZ : 2 * MZ] = -sin.T
    table[points:, MZ : 2 * MZ] = cos.T
    return const(table)


def z_inverse_table(points, first, other):
    cos, sin = z_parts(points, first, other)
    table = np.zeros((128, 2 * points))
    table[:MZ, :points] = cos
    table[MZ : 2 * MZ, :points] = -sin
    table[:MZ, points:] = sin
    table[MZ : 2 * MZ, points:] = cos
    return const(table)


def x_blocks(points, sign, scale):
    real, imag = wave(points, MX, sign, scale)
    table = np.stack([np.stack([real, -imag]), np.stack([imag, real])])
    return table.reshape(2, 2, MX // OCT, OCT, points)


def x_forward_table(points, parts, wide, cells_x, scale, turned=False):
    table = x_blocks(points, -1.0, scale)
    if turned:
        table = np.stack([table[1], -table[0]])
    table = table.reshape(2, 2, MX // OCT, OCT, wide, cells_x)
    table = np.broadcast_to(table, (parts,) + table.shape)
    table = np.einsum("nrsjmwa->ajrmnws", table)
    return table.reshape(cells_x * 2 * MX, parts * wide * 2)


def x_inverse_table(points, wide, cells_x, scale):
    table = x_blocks(points, 1.0, scale).reshape(2, 2, MX // OCT, OCT, wide, cells_x)
    return const(np.einsum("rsjmwa->awrjsm", table).reshape(cells_x * wide * 2, 2 * MX))


def lane_masks(cells_x):
    lanes = np.arange(C * cells_x) % cells_x
    masks = np.zeros((8, C * cells_x), np.float32)
    masks[:cells_x] = lanes[None, :] == np.arange(cells_x)[:, None]
    return jnp.asarray(masks)


def octet_of_rows():
    return np.arange(2 * MX) % OCT


def forward_transform(get_rows, y_table, z_table, out_ref, held, turned, cells_x):
    rows = cells_x * MY
    together = 4

    def channels(step, carry):
        for offset in range(together):
            c = step * together + offset
            part = mm(y_table, get_rows(c)).astype(BF16)
            both = jnp.concatenate([part[:rows], part[rows:]], axis=1)
            held[pl.ds(pl.multiple_of(c * rows, 8), rows), :] = mm(both, z_table)
        return carry

    lax.fori_loop(0, C // together, channels, 0)
    for q in range(MY):
        block = held[pl.ds(q, C * cells_x, stride=MY), :]
        turned[pl.ds(q, 2 * MZ, stride=MY), :] = block.T[: 2 * MZ]
    pairs = out_ref.shape[2]
    for target in range(out_ref.shape[0]):
        for part in range(2):
            begin = part * MZ * MY + target * pairs
            out_ref[target, part] = turned[begin : begin + pairs, :].astype(BF16)


def inverse_transform(in_ref, y_table, z_table, put_rows, held, turned, cells_x):
    rows = cells_x * MY
    together = 4
    pairs = in_ref.shape[2]
    points = z_table.shape[1] // 2
    lanes = held.shape[1]
    for source in range(in_ref.shape[0]):
        for part in range(2):
            begin = part * MZ * MY + source * pairs
            turned[begin : begin + pairs, :] = in_ref[source, part].astype(F32)
    for q in range(MY):
        block = turned[pl.ds(q, 2 * MZ, stride=MY), :]
        padded = jnp.concatenate([block, jnp.zeros((lanes - 2 * MZ, block.shape[1]), F32)], axis=0)
        held[pl.ds(q, C * cells_x, stride=MY), :] = padded.T

    def channels(step, carry):
        for offset in range(together):
            c = step * together + offset
            block = held[pl.ds(pl.multiple_of(c * rows, 8), rows), :].astype(BF16)
            both = mm(block, z_table).astype(BF16)
            stacked = jnp.concatenate([both[:, :points], both[:, points:]], axis=0)
            put_rows(c, mm(y_table, stacked))
        return carry

    lax.fori_loop(0, C // together, channels, 0)


def forward_kernel(cells_x, field, y_tables, z_table, out_ref, held, turned):
    y_table = y_tables[lax.axis_index("narrow")]
    forward_transform(
        lambda c: field[c], y_table, z_table[...], out_ref, held, turned, cells_x
    )


def tall_mixer(spread, mixer, mask):
    wide = mm(spread, mixer).astype(BF16)
    return (mm_nt(wide, spread).astype(BF16)) * mask


def mixed_field(table, field, begin, band):
    depth = field.shape[2]
    blocks = [field[:, pl.ds(begin + half * band, band), :] for half in range(2)]
    flat = [block.reshape(C * band, depth) for block in blocks]
    product = mm(table, jnp.concatenate(flat, axis=1))
    return [product[:, half * depth : (half + 1) * depth].reshape(C, band, depth) for half in range(2)]


def middle_kernel(
    cells_x, band, arrived, field, upstream, spread, mixer, mask, bias,
    y_back, z_back, y_dual, z_dual,
    layer_out, slope, out_ref, held, turned, spectral,
):
    me = lax.axis_index("narrow")

    def put(c, rows):
        spectral[c] = rows

    inverse_transform(arrived, y_back[me], z_back[...], put, held, turned, cells_x)
    table = tall_mixer(spread[...], mixer[...], mask[...])
    offset = bias[...][:, :, None]
    alpha = math.sqrt(2.0 / math.pi)
    cubic = alpha * 0.044715

    def bands(step, carry):
        begin = pl.multiple_of(step * 2 * band, 2 * band)
        linear = mixed_field(table, field, begin, band)
        for half in range(2):
            where = pl.ds(begin + half * band, band)
            v = spectral[:, where, :] + (linear[half] + offset)
            square = v * v
            t = jnp.tanh(v * (alpha + cubic * square))
            gate = 0.5 + 0.5 * t
            layer_out[:, where, :] = (v * gate).astype(BF16)
            rise = (0.5 * v) * (1.0 - t * t) * (alpha + (3.0 * cubic) * square)
            grad = upstream[:, where, :].astype(F32) * (gate + rise)
            slope[:, where, :] = grad.astype(BF16)
        return carry

    lax.fori_loop(0, field.shape[1] // (2 * band), bands, 0)
    forward_transform(
        lambda c: slope[c], y_dual[me], z_dual[...], out_ref, held, turned, cells_x
    )


def final_kernel(
    cells_x, band, arrived, slope, spread, mixer, mask, y_back, z_back, out_ref, held, turned,
    spectral,
):
    me = lax.axis_index("narrow")

    def put(c, rows):
        spectral[c] = rows

    inverse_transform(arrived, y_back[me], z_back[...], put, held, turned, cells_x)
    table = tall_mixer(spread[...], mixer[...], mask[...])

    def bands(step, carry):
        begin = pl.multiple_of(step * 2 * band, 2 * band)
        linear = mixed_field(table, slope, begin, band)
        for half in range(2):
            where = pl.ds(begin + half * band, band)
            out_ref[:, where, :] = (spectral[:, where, :] + linear[half]).astype(BF16)
        return carry

    lax.fori_loop(0, slope.shape[1] // (2 * band), bands, 0)


def unpack_pairs(arrived, loose):
    pairs = arrived.shape[2]
    for source in range(arrived.shape[0]):
        for part in range(2):
            begin = (source * 2 + part) * pairs
            loose[begin : begin + pairs, :] = arrived[source, part].astype(F32)


def pick_cells(product, masks, cells_x, begin=0):
    rows = product.shape[0] // cells_x if begin is None else 2 * MX
    total = None
    for a in range(cells_x):
        low = (begin or 0) + a * rows
        term = product[low : low + rows] * masks[a : a + 1]
        total = term if total is None else total + term
    return total


def send_pairs(gathered, out_ref, wide):
    pairs = out_ref.shape[2]
    for target in range(out_ref.shape[0]):
        for part in range(2):
            begin = ((target % wide) * 2 + part) * pairs
            out_ref[target, part] = gathered[begin : begin + pairs, :].astype(BF16)


def mix_kernel(
    cells_x, wide, group, arrived, weights, x_table, x_back, masks, copies, octets, picks,
    out_ref, spectrum_t, loose, gathered,
):
    step = pl.program_id(0)
    pairs = arrived.shape[2]
    sources = arrived.shape[0] * 2

    @pl.when(step == 0)
    def _():
        unpack_pairs(arrived, loose)

    lanes = masks[...]
    for offset in range(group):
        pair = step * group + offset
        data = loose[pl.ds(pair, sources, stride=pairs), :].astype(BF16)
        chosen = pick_cells(mm(x_table[...], data), lanes, cells_x).astype(BF16)
        spectrum_t[offset] = mm_nt(picks[...], chosen).astype(BF16)
        diagonal = mm(chosen, copies[...]).astype(BF16) * octets[...]
        rows = []
        for j in range(MX // OCT):
            low = offset * MX * C + j * OCT * C
            product = mm(diagonal[2 * OCT * j : 2 * OCT * (j + 1)], weights[low : low + OCT * C, :])
            top, bottom = product[:OCT], product[OCT:]
            rows.append(top[:, :C] - bottom[:, C:])
            rows.append(top[:, C:] + bottom[:, :C])
        mixed = jnp.concatenate(rows, axis=0).astype(BF16)
        back = mm(x_back[...], mm(mixed, picks[...]).astype(BF16))
        gathered[pl.ds(pair, 2 * wide, stride=pairs), :] = pick_cells(back, lanes, cells_x, None)

    @pl.when(step == pl.num_programs(0) - 1)
    def _():
        send_pairs(gathered, out_ref, wide)


def grad_kernel(
    cells_x, wide, group, arrived, weights, spectrum_t, x_table, x_back, masks, sides, octets,
    octets_t, shrink, out_ref, weight_grad, loose, gathered,
):
    step = pl.program_id(0)
    pairs = arrived.shape[2]
    sources = arrived.shape[0] * 2

    @pl.when(step == 0)
    def _():
        unpack_pairs(arrived, loose)

    lanes = masks[...]
    for offset in range(group):
        pair = step * group + offset
        data = loose[pl.ds(pair, sources, stride=pairs), :].astype(BF16)
        product = mm(x_table[...], data)
        straight = pick_cells(product, lanes, cells_x).astype(BF16)
        turned = pick_cells(product, lanes, cells_x, 2 * MX * cells_x).astype(BF16)
        stacked = mm(jnp.concatenate([straight, turned], axis=1), sides[...]).astype(BF16)
        tall = jnp.concatenate([spectrum_t[offset]] * MX, axis=0) * octets_t[...]
        low = offset * MX * C
        weight_grad[low : low + MX * C, :] = mm(tall, stacked)
        rows = []
        for j in range(MX // OCT):
            block = weights[low + j * OCT * C : low + (j + 1) * OCT * C, :]
            rows.append(mm_nt(stacked[2 * OCT * j : 2 * OCT * (j + 1)], block))
        coeff = jnp.concatenate(rows, axis=0).astype(BF16) * octets[...]
        back = mm(x_back[...], mm(coeff, shrink[...]).astype(BF16))
        gathered[pl.ds(pair, 2 * wide, stride=pairs), :] = pick_cells(back, lanes, cells_x, None)

    @pl.when(step == pl.num_programs(0) - 1)
    def _():
        send_pairs(gathered, out_ref, wide)


def exchange(blocks):
    return lax.all_to_all(blocks, ("narrow", "wide"), split_axis=0, concat_axis=0, tiled=True)


def whole_spec(shape):
    return pl.BlockSpec(shape, lambda *_: (0,) * len(shape))


def body(plume_state, spectral_weight, channel_mixer, channel_bias, upstream_grad):
    row_count, cells_x, cells_y, depth = plume_state.shape
    wide = lax.axis_size("wide")
    parts = lax.axis_size("narrow")
    span_x = cells_x * wide
    span_y = cells_y * parts
    flat = cells_x * cells_y
    lanes = C * cells_x
    targets = parts * wide
    pairs = spectral_weight.shape[1]
    band = 16
    group = max(g for g in (4, 3, 2, 1) if pairs % g == 0)
    down = 1.0 / math.sqrt(depth)
    z_fwd = z_forward_table(depth, down, down)
    z_fwd_back = z_inverse_table(depth, down, down)
    first, other = 1.0 / math.sqrt(2 * MZ), 2.0 / math.sqrt(2 * MZ)
    z_inv = z_inverse_table(depth, first, other)
    z_inv_back = z_forward_table(depth, first, other)
    y_fwd = y_forward_table(span_y, parts, cells_x, 1.0 / math.sqrt(span_y))
    y_inv = y_inverse_table(span_y, parts, cells_x, 1.0 / math.sqrt(MY))
    y_dual_inv = y_forward_table(span_y, parts, cells_x, 1.0 / math.sqrt(MY))
    y_dual_fwd = y_inverse_table(span_y, parts, cells_x, 1.0 / math.sqrt(span_y))
    x_fwd = const(x_forward_table(span_x, parts, wide, cells_x, 1.0 / math.sqrt(span_x)))
    x_inv = x_inverse_table(span_x, wide, cells_x, 1.0 / math.sqrt(MX))
    scale = 1.0 / math.sqrt(MX)
    x_dual_inv = const(
        np.concatenate(
            [x_forward_table(span_x, parts, wide, cells_x, scale, turn) for turn in (False, True)]
        )
    )
    x_dual_fwd = x_inverse_table(span_x, wide, cells_x, 1.0 / math.sqrt(span_x))
    masks = lane_masks(cells_x)
    lane_c = np.arange(lanes) // cells_x
    picks_np = np.arange(C)[:, None] == lane_c[None, :]
    picks = const(picks_np)
    copies_np = np.tile(picks_np.T, (1, OCT))
    copies = const(copies_np)
    shrink = const(copies_np.T)
    octets_np = octet_of_rows()[:, None] == (np.arange(OCT * C) // C)[None, :]
    octets = const(octets_np)
    row_mode = (np.arange(2 * MX) // (2 * OCT)) * OCT + np.arange(2 * MX) % OCT
    octets_t = const((np.arange(MX * C) // C)[:, None] == row_mode[None, :])
    sides_np = np.zeros((2 * lanes, 2 * C))
    sides_np[:lanes, :C] = picks_np.T
    sides_np[lanes:, C:] = picks_np.T
    sides = const(sides_np)
    spread = const((np.arange(C * band) // band)[:, None] == np.arange(C)[None, :])
    band_index = np.arange(C * band) % band
    band_mask = const(band_index[:, None] == band_index[None, :])

    params = pltpu.CompilerParams(vmem_limit_bytes=VMEM_LIMIT)
    message = jax.ShapeDtypeStruct((targets, 2, pairs, lanes), BF16)
    held = pltpu.VMEM((lanes * MY, 128), F32)
    turned = pltpu.VMEM((2 * MZ * MY, lanes), F32)
    spectral = pltpu.VMEM((C, flat, depth), F32)
    loose = pltpu.VMEM((targets * 2 * pairs, lanes), F32)
    gathered = pltpu.VMEM((2 * wide * pairs, lanes), F32)
    field = plume_state.reshape(C, flat, depth)
    upstream = upstream_grad.reshape(C, flat, depth)
    weights = spectral_weight.reshape(pairs * MX * C, 2 * C)
    field_shape = jax.ShapeDtypeStruct((C, flat, depth), BF16)
    weight_spec = pl.BlockSpec((group * MX * C, 2 * C), lambda i: (i, 0))
    spectrum_spec = pl.BlockSpec((group, C, 2 * MX), lambda i: (i, 0, 0))

    sent = pl.pallas_call(
        functools.partial(forward_kernel, cells_x),
        out_shape=message,
        scratch_shapes=[held, turned],
        compiler_params=params,
    )(field, y_fwd, z_fwd)
    arrived = exchange(sent)

    operands = (x_fwd, x_inv, masks, copies, octets, picks)
    sent, spectrum_t = pl.pallas_call(
        functools.partial(mix_kernel, cells_x, wide, group),
        grid=(pairs // group,),
        in_specs=[whole_spec(message.shape), weight_spec] + [whole_spec(t.shape) for t in operands],
        out_specs=[whole_spec(message.shape), spectrum_spec],
        out_shape=[message, jax.ShapeDtypeStruct((pairs, C, 2 * MX), BF16)],
        scratch_shapes=[loose, gathered],
        compiler_params=params,
    )(arrived, weights, *operands)
    arrived = exchange(sent)

    layer_out, slope, sent = pl.pallas_call(
        functools.partial(middle_kernel, cells_x, band),
        out_shape=[field_shape, field_shape, message],
        scratch_shapes=[held, turned, spectral],
        compiler_params=params,
    )(
        arrived, field, upstream, spread, channel_mixer.T, band_mask, channel_bias[:, None],
        y_inv, z_inv, y_dual_inv, z_inv_back,
    )
    arrived = exchange(sent)

    operands = (x_dual_inv, x_dual_fwd, masks, sides, octets, octets_t, shrink)
    sent, weight_grad = pl.pallas_call(
        functools.partial(grad_kernel, cells_x, wide, group),
        grid=(pairs // group,),
        in_specs=[whole_spec(message.shape), weight_spec, spectrum_spec]
        + [whole_spec(t.shape) for t in operands],
        out_specs=[whole_spec(message.shape), weight_spec],
        out_shape=[message, jax.ShapeDtypeStruct(weights.shape, F32)],
        scratch_shapes=[loose, gathered],
        compiler_params=params,
    )(arrived, weights, spectrum_t, *operands)
    arrived = exchange(sent)

    state_grad = pl.pallas_call(
        functools.partial(final_kernel, cells_x, band),
        out_shape=field_shape,
        scratch_shapes=[held, turned, spectral],
        compiler_params=params,
    )(arrived, slope, spread, channel_mixer, band_mask, y_dual_fwd, z_fwd_back)
    return (
        layer_out.reshape(plume_state.shape),
        state_grad.reshape(plume_state.shape),
        weight_grad.reshape(spectral_weight.shape),
    )


def solution(mesh):
    in_specs = (
        P("groups", "wide", "narrow", None),
        P("narrow", "wide", None, None, None),
        P(),
        P(),
        P("groups", "wide", "narrow", None),
    )
    out_specs = (
        P("groups", "wide", "narrow", None),
        P("groups", "wide", "narrow", None),
        P("narrow", "wide", "groups", None, None),
    )
    return jax.shard_map(body, mesh=mesh, in_specs=in_specs, out_specs=out_specs, check_vma=False)
```

profile of v0, /device:TPU:0, one launch (start us, length us, event | category | flops | bytes accessed | tf_op | source)
XLA Modules:
  0.0 152.8 jit_solution(2053936927626976877)
XLA Ops:
  0.6 1.6 %copy-done = bf16[32,4,64,128]{3,2,1,0:T(8,128)(2,1)S(1)} copy-done((bf16[32,4,64,128]{3,2,1,0:T(8,128)(2,1)S(1)}, bf16[32,4,64,128]{3,2,1,0:T(8,128)(2,1)}, u32[]{:S(2)}) %copy-start) | copy-done | bytes 2097176
  2.2 0.9 copy-done.7
  3.2 0.8 copy-done.16
  4.0 0.0 copy-start.21
  4.0 0.0 copy-start.22
  4.0 7.1 %shard_map.265 = bf16[16,2,36,128]{3,2,1,0:T(8,128)(2,1)S(1)} custom-call(bf16[32,256,128]{2,1,0:T(8,128)(2,1)S(1)} %bitcast.9, bf16[2,192,256]{2,1,0:T(8,128)(2,1)S(1)} %copy-done.7, bf16[256,128]{1,0:T(8,128)(2,1)S(1)} %copy-done.16), custom_call_target="tpu_custom_call" | custom-call | tf_op jit(solution)/shard_map/pallas_call | solution.py:416
  11.1 0.2 copy.31
  11.4 18.2 %all_to_all.20 = bf16[16,2,36,128]{3,1,2,0:T(2,128)(2,1)S(1)} all-to-all(bf16[16,2,36,128]{3,1,2,0:T(2,128)(2,1)S(1)} %copy.31), channel_id=1, replica_groups=mesh['groups'=2,'wide'=8,'narrow'=2] {'narrow','wide'}, dimensions={0} | all-to-all | bytes 589824 | tf_op jit(solution)/shard_map/all_to_all | solution.py:345
  29.7 0.0 copy-start.3
  29.7 0.0 copy-start.5
  29.8 0.0 copy-start.13
  29.8 0.0 copy-start.14
  29.8 25.2 %shard_map.266 = (bf16[16,2,36,128]{3,2,1,0:T(8,128)(2,1)S(1)}, bf16[36,32,48]{2,1,0:T(8,128)(2,1)S(1)}) custom-call(bf16[16,2,36,128]{3,2,1,0:T(8,128)(2,1)S(1)} %copy.32.arrived, bf16[27648,64]{1,0:T(8,128)(2,1)} %bitcast.11, bf16[192,32]{1,0:T(8,128)(2,1)S(1)} %copy-done.17, bf16[64,48]{1,0:T(8,128)(2,1)S(1)} %copy-done.21, f32[8,128]{1,0:T(8,128)S(1)} %copy-done.19, ...), custom_call_target="tpu_custom_call" | custom-call | tf_op jit(solution)/shard_map/pallas_call | solution.py:425
  55.0 0.0 copy-start.1
  55.0 0.9 copy.33
  56.0 3.5 %all-to-all-start.1 = ((bf16[16,2,36,128]{3,1,2,0:T(2,128)(2,1)}), bf16[16,2,36,128]{3,1,2,0:T(2,128)(2,1)S(1)}, u32[]{:S(2)}, u32[]{:S(2)}) async-start(bf16[16,2,36,128]{3,1,2,0:T(2,128)(2,1)} %copy.33), calls=%async_computation.1 | async-start | bytes 589824 | tf_op jit(solution)/shard_map/all_to_all | solution.py:345
  59.5 0.1 copy.34
  59.6 0.1 copy.36.bias
  59.7 10.8 %all-to-all-done.1 = bf16[16,2,36,128]{3,1,2,0:T(2,128)(2,1)S(1)} async-done(((bf16[16,2,36,128]{3,1,2,0:T(2,128)(2,1)}), bf16[16,2,36,128]{3,1,2,0:T(2,128)(2,1)S(1)}, u32[]{:S(2)}, u32[]{:S(2)}) %all-to-all-start.1) | async-done | bytes 294944 | tf_op jit(solution)/shard_map/all_to_all | solution.py:345
  70.6 0.0 copy-start.6
  70.6 0.0 copy-start.8
  70.6 0.0 copy-start.11
  70.7 0.0 copy-start.20
  70.7 19.7 %shard_map.267 = (bf16[32,256,128]{2,1,0:T(8,128)(2,1)}, bf16[32,256,128]{2,1,0:T(8,128)(2,1)S(1)}, bf16[16,2,36,128]{3,2,1,0:T(8,128)(2,1)S(1)}) custom-call(bf16[16,2,36,128]{3,2,1,0:T(8,128)(2,1)S(1)} %copy.35.arrived, bf16[32,256,128]{2,1,0:T(8,128)(2,1)} %bitcast.8, bf16[32,256,128]{2,1,0:T(8,128)(2,1)} %bitcast.13, bf16[512,32]{1,0:T(8,128)(2,1)S(1)} %copy-done.2, ...), custom_call_target="tpu_custom_call" | custom-call | tf_op jit(solution)/shard_map/pallas_call | solution.py:436
  90.4 0.2 copy.37
  90.6 13.6 %all_to_all.21 = bf16[16,2,36,128]{3,1,2,0:T(2,128)(2,1)S(1)} all-to-all(bf16[16,2,36,128]{3,1,2,0:T(2,128)(2,1)S(1)} %copy.37), channel_id=1, replica_groups=mesh['groups'=2,'wide'=8,'narrow'=2] {'narrow','wide'}, dimensions={0} | all-to-all | bytes 589824 | tf_op jit(solution)/shard_map/all_to_all | solution.py:345
  104.3 0.0 copy-start.4
  104.3 0.0 copy-start.10
  104.4 24.9 %shard_map.268 = (bf16[16,2,36,128]{3,2,1,0:T(8,128)(2,1)S(1)}, f32[27648,64]{1,0:T(8,128)}) custom-call(bf16[16,2,36,128]{3,2,1,0:T(8,128)(2,1)S(1)} %copy.38.arrived, bf16[27648,64]{1,0:T(8,128)(2,1)} %bitcast.12, bf16[36,32,48]{2,1,0:T(8,128)(2,1)S(1)} %get-tuple-element.13.spectrum_t, bf16[384,32]{1,0:T(8,128)(2,1)S(1)} %copy-done.8, ...), custom_call_target="tpu_custom_call" | custom-call | tf_op jit(solution)/shard_map/pallas_call | solution.py:448
  129.3 0.2 copy.39
  129.5 13.6 %all_to_all.22 = bf16[16,2,36,128]{3,1,2,0:T(2,128)(2,1)S(1)} all-to-all(bf16[16,2,36,128]{3,1,2,0:T(2,128)(2,1)S(1)} %copy.39), channel_id=1, replica_groups=mesh['groups'=2,'wide'=8,'narrow'=2] {'narrow','wide'}, dimensions={0} | all-to-all | bytes 589824 | tf_op jit(solution)/shard_map/all_to_all | solution.py:345
  143.2 9.6 %shard_map.269 = bf16[32,256,128]{2,1,0:T(8,128)(2,1)} custom-call(bf16[16,2,36,128]{3,2,1,0:T(8,128)(2,1)S(1)} %copy.40.arrived, bf16[32,256,128]{2,1,0:T(8,128)(2,1)S(1)} %get-tuple-element.15.slope, bf16[512,32]{1,0:T(8,128)(2,1)S(1)} %copy-done.2, bf16[32,32]{1,0:T(8,128)(2,1)S(1)} %copy-done.18, bf16[512,512]{1,0:T(8,128)(2,1)S(1)} %copy-done.1, ...), custom_call_target="tpu_custom_call" | custom-call | tf_op jit(solution)/shard_map/pallas_call | solution.py:460
  (36 shorter events, 0.3 us)
Async XLA Ops:
  0.6 1.6 %copy-start = (bf16[32,4,64,128]{3,2,1,0:T(8,128)(2,1)S(1)}, bf16[32,4,64,128]{3,2,1,0:T(8,128)(2,1)}, u32[]{:S(2)}) copy-start(bf16[32,4,64,128]{3,2,1,0:T(8,128)(2,1)} %param.26) | copy-start | bytes 6291460
  2.2 0.9 copy-start.7
  3.2 0.8 copy-start.16
  4.0 25.6 %copy-start.9 = (bf16[48,256]{1,0:T(8,128)(2,1)S(1)}, bf16[48,256]{1,0:T(8,128)(2,1)}, u32[]{:S(2)}) copy-start(bf16[48,256]{1,0:T(8,128)(2,1)} %constant.71.octets) | copy-start | bytes 73732
  4.0 25.7 %copy-start.15 = (bf16[128,256]{1,0:T(8,128)(2,1)S(1)}, bf16[128,256]{1,0:T(8,128)(2,1)}, u32[]{:S(2)}) copy-start(bf16[128,256]{1,0:T(8,128)(2,1)} %constant.70.copies) | copy-start | bytes 196612
  4.0 25.7 %copy-start.17 = (bf16[192,32]{1,0:T(8,128)(2,1)S(1)}, bf16[192,32]{1,0:T(8,128)(2,1)}, u32[]{:S(2)}) copy-start(bf16[192,32]{1,0:T(8,128)(2,1)} %constant.68.x_table) | copy-start | bytes 36868
  4.0 25.7 %copy-start.19 = (f32[8,128]{1,0:T(8,128)S(1)}, f32[8,128]{1,0:T(8,128)}, u32[]{:S(2)}) copy-start(f32[8,128]{1,0:T(8,128)} %constant.54.clone.masks) | copy-start | bytes 12292
  4.0 25.7 %copy-start.21 = (bf16[64,48]{1,0:T(8,128)(2,1)S(1)}, bf16[64,48]{1,0:T(8,128)(2,1)}, u32[]{:S(2)}) copy-start(bf16[64,48]{1,0:T(8,128)(2,1)} %constant.69.x_back) | copy-start | bytes 18436
  4.0 25.7 %copy-start.22 = (bf16[32,128]{1,0:T(8,128)(2,1)S(1)}, bf16[32,128]{1,0:T(8,128)(2,1)}, u32[]{:S(2)}) copy-start(bf16[32,128]{1,0:T(8,128)(2,1)} %constant.72.picks) | copy-start | bytes 24580
  29.7 29.8 %copy-start.18 = (bf16[32,32]{1,0:T(8,128)(2,1)S(1)}, bf16[32,32]{1,0:T(8,128)(2,1)}, u32[]{:S(2)}) copy-start(bf16[32,32]{1,0:T(8,128)(2,1)} %mixer.1) | copy-start | bytes 6148
  29.7 29.9 %copy-start.23 = (f32[32]{0:T(128)S(1)}, f32[32]{0:T(128)}, u32[]{:S(2)}) copy-start(f32[32]{0:T(128)} %param.29) | copy-start | bytes 388
  29.7 40.8 %copy-start.2 = (bf16[512,32]{1,0:T(8,128)(2,1)S(1)}, bf16[512,32]{1,0:T(8,128)(2,1)}, u32[]{:S(2)}) copy-start(bf16[512,32]{1,0:T(8,128)(2,1)} %constant.73.spread) | copy-start | bytes 98308
  29.7 40.8 %copy-start.3 = (bf16[2,256,192]{2,1,0:T(8,128)(2,1)S(1)}, bf16[2,256,192]{2,1,0:T(8,128)(2,1)}, u32[]{:S(2)}) copy-start(bf16[2,256,192]{2,1,0:T(8,128)(2,1)} %constant.75.y_back) | copy-start | bytes 589828
  29.7 40.8 %copy-start.5 = (bf16[2,192,256]{2,1,0:T(8,128)(2,1)S(1)}, bf16[2,192,256]{2,1,0:T(8,128)(2,1)}, u32[]{:S(2)}) copy-start(bf16[2,192,256]{2,1,0:T(8,128)(2,1)} %constant.77.y_dual) | copy-start | bytes 589828
  29.8 40.8 %copy-start.13 = (bf16[256,128]{1,0:T(8,128)(2,1)S(1)}, bf16[256,128]{1,0:T(8,128)(2,1)}, u32[]{:S(2)}) copy-start(bf16[256,128]{1,0:T(8,128)(2,1)} %constant.78.z_dual) | copy-start | bytes 196612
  29.8 40.8 %copy-start.14 = (bf16[128,256]{1,0:T(8,128)(2,1)S(1)}, bf16[128,256]{1,0:T(8,128)(2,1)}, u32[]{:S(2)}) copy-start(bf16[128,256]{1,0:T(8,128)(2,1)} %constant.76.z_back) | copy-start | bytes 196612
  55.0 15.6 %copy-start.1 = (bf16[512,512]{1,0:T(8,128)(2,1)S(1)}, bf16[512,512]{1,0:T(8,128)(2,1)}, u32[]{:S(2)}) copy-start(bf16[512,512]{1,0:T(8,128)(2,1)} %constant.74.mask) | copy-start | bytes 1572868
  56.0 14.5 %all-to-all-start.1 = ((bf16[16,2,36,128]{3,1,2,0:T(2,128)(2,1)}), bf16[16,2,36,128]{3,1,2,0:T(2,128)(2,1)S(1)}, u32[]{:S(2)}, u32[]{:S(2)}) async-start(bf16[16,2,36,128]{3,1,2,0:T(2,128)(2,1)} %copy.33), calls=%async_computation.1 | async-start | bytes 589824 | tf_op jit(solution)/shard_map/all_to_all | solution.py:345
  70.6 33.7 %copy-start.6 = (bf16[768,48]{1,0:T(8,128)(2,1)S(1)}, bf16[768,48]{1,0:T(8,128)(2,1)}, u32[]{:S(2)}) copy-start(bf16[768,48]{1,0:T(8,128)(2,1)} %constant.82.octets_t) | copy-start | bytes 221188
  70.6 33.7 %copy-start.8 = (bf16[384,32]{1,0:T(8,128)(2,1)S(1)}, bf16[384,32]{1,0:T(8,128)(2,1)}, u32[]{:S(2)}) copy-start(bf16[384,32]{1,0:T(8,128)(2,1)} %constant.79.x_table) | copy-start | bytes 73732
  70.6 33.7 %copy-start.11 = (bf16[256,128]{1,0:T(8,128)(2,1)S(1)}, bf16[256,128]{1,0:T(8,128)(2,1)}, u32[]{:S(2)}) copy-start(bf16[256,128]{1,0:T(8,128)(2,1)} %constant.83.shrink) | copy-start | bytes 196612
  70.6 33.7 %copy-start.12 = (bf16[256,64]{1,0:T(8,128)(2,1)S(1)}, bf16[256,64]{1,0:T(8,128)(2,1)}, u32[]{:S(2)}) copy-start(bf16[256,64]{1,0:T(8,128)(2,1)} %constant.81.sides) | copy-start | bytes 98308
  70.7 33.7 %copy-start.20 = (bf16[64,48]{1,0:T(8,128)(2,1)S(1)}, bf16[64,48]{1,0:T(8,128)(2,1)}, u32[]{:S(2)}) copy-start(bf16[64,48]{1,0:T(8,128)(2,1)} %constant.80.x_back) | copy-start | bytes 18436
  104.3 38.9 %copy-start.4 = (bf16[2,256,192]{2,1,0:T(8,128)(2,1)S(1)}, bf16[2,256,192]{2,1,0:T(8,128)(2,1)}, u32[]{:S(2)}) copy-start(bf16[2,256,192]{2,1,0:T(8,128)(2,1)} %constant.84.y_back) | copy-start | bytes 589828
  104.3 38.9 %copy-start.10 = (bf16[128,256]{1,0:T(8,128)(2,1)S(1)}, bf16[128,256]{1,0:T(8,128)(2,1)}, u32[]{:S(2)}) copy-start(bf16[128,256]{1,0:T(8,128)(2,1)} %constant.85.z_back) | copy-start | bytes 196612
where the time goes:
time: 153 us
  Pallas kernels  86.6 us (57%)
  blocking collectives  45.5 us (30%)
  waiting for transfers between devices  10.8 us (7%)
  local copies, waits for them, and re-layouts  5.46 us (4%)
  starting transfers between devices  3.54 us (2%)
    all_to_all x3, blocking collectives, exchange(): lax.all_to_all(blocks, ('narrow', 'wide'), split_axis=0, concat_axis=0, t...  45.5 us
    pallas_call x1, Pallas kernels, body(): pl.pallas_call(functools.partial(mix_kernel, cells_x, wide, group), grid=...  25.2 us
    pallas_call x1, Pallas kernels, body(): pl.pallas_call(functools.partial(grad_kernel, cells_x, wide, group), grid...  24.9 us
    pallas_call x1, Pallas kernels, body(): pl.pallas_call(functools.partial(middle_kernel, cells_x, band), out_shape...  19.7 us
    all_to_all x1, waiting for transfers between devices, exchange(): lax.all_to_all(blocks, ('narrow', 'wide'), split_axis=0, concat_axis=0, t...  10.8 us
    pallas_call x1, Pallas kernels, body(): pl.pallas_call(functools.partial(final_kernel, cells_x, band), out_shape=...  9.6 us
    pallas_call x1, Pallas kernels, body(): pl.pallas_call(functools.partial(forward_kernel, cells_x), out_shape=mess...  7.08 us
    unnamed x49, local copies, waits for them, and re-layouts  3.57 us
  transfers between devices with their start and end apart: 1, of which 1 were waited for; matrix products, arithmetic and copies ran while one was open for 0% of the time, Pallas kernels for 0%

commit v1 on v0

--- a/solution.py
+++ b/solution.py
@@ -94,20 +94,18 @@
         table = np.stack([table[1], -table[0]])
     table = table.reshape(2, 2, MX // OCT, OCT, wide, cells_x)
     table = np.broadcast_to(table, (parts,) + table.shape)
-    table = np.einsum("nrsjmwa->ajrmnws", table)
-    return table.reshape(cells_x * 2 * MX, parts * wide * 2)
+    table = np.einsum("nrsjmwa->jrmanws", table)
+    return table.reshape(2 * MX, cells_x * parts * wide * 2)
 
 
 def x_inverse_table(points, wide, cells_x, scale):
     table = x_blocks(points, 1.0, scale).reshape(2, 2, MX // OCT, OCT, wide, cells_x)
-    return const(np.einsum("rsjmwa->awrjsm", table).reshape(cells_x * wide * 2, 2 * MX))
-
-
-def lane_masks(cells_x):
-    lanes = np.arange(C * cells_x) % cells_x
-    masks = np.zeros((8, C * cells_x), np.float32)
-    masks[:cells_x] = lanes[None, :] == np.arange(cells_x)[:, None]
-    return jnp.asarray(masks)
+    return const(np.einsum("rsjmwa->wrajsm", table).reshape(wide * 2, cells_x * 2 * MX))
+
+
+def cell_mask(cells_x, rows):
+    owner = np.arange(cells_x * rows) // rows
+    return const(owner[:, None] == (np.arange(C * cells_x) % cells_x)[None, :])
 
 
 def octet_of_rows():
@@ -252,14 +250,26 @@
             loose[begin : begin + pairs, :] = arrived[source, part].astype(F32)
 
 
-def pick_cells(product, masks, cells_x, begin=0):
-    rows = product.shape[0] // cells_x if begin is None else 2 * MX
-    total = None
-    for a in range(cells_x):
-        low = (begin or 0) + a * rows
-        term = product[low : low + rows] * masks[a : a + 1]
-        total = term if total is None else total + term
-    return total
+def to_modes(loose, x_table, cell_rows, first, group, pairs, cells_x):
+    count = loose.shape[0] // pairs
+    blocks = []
+    for offset in range(group):
+        data = loose[pl.ds(first + offset, count, stride=pairs), :].astype(BF16)
+        blocks.append(jnp.concatenate([data] * cells_x, axis=0) * cell_rows)
+    return mm(x_table, jnp.concatenate(blocks, axis=1)).astype(BF16)
+
+
+def from_modes(modes, x_back, cell_rows, gathered, first, group, pairs, cells_x):
+    rows = 2 * MX
+    lanes = modes.shape[1]
+    blocks = []
+    for offset in range(group):
+        data = modes[offset * rows : (offset + 1) * rows]
+        blocks.append(jnp.concatenate([data] * cells_x, axis=0) * cell_rows)
+    back = mm(x_back, jnp.concatenate(blocks, axis=1))
+    for offset in range(group):
+        where = pl.ds(first + offset, x_back.shape[0], stride=pairs)
+        gathered[where, :] = back[:, offset * lanes : (offset + 1) * lanes]
 
 
 def send_pairs(gathered, out_ref, wide):
@@ -270,35 +280,46 @@
             out_ref[target, part] = gathered[begin : begin + pairs, :].astype(BF16)
 
 
+def per_pair(array, group, low, high):
+    lanes = array.shape[1] // group
+    parts = [array[low:high, n * lanes : (n + 1) * lanes] for n in range(group)]
+    return jnp.concatenate(parts, axis=0)
+
+
 def mix_kernel(
-    cells_x, wide, group, arrived, weights, x_table, x_back, masks, copies, octets, picks,
-    out_ref, spectrum_t, loose, gathered,
+    cells_x, wide, group, arrived, weights, x_table, x_back, source_rows, mode_rows, copies,
+    octets, picks, doubled, out_ref, spectrum_t, loose, gathered,
 ):
     step = pl.program_id(0)
     pairs = arrived.shape[2]
-    sources = arrived.shape[0] * 2
+    rows = 2 * MX
+    first = step * group
 
     @pl.when(step == 0)
     def _():
         unpack_pairs(arrived, loose)
 
-    lanes = masks[...]
-    for offset in range(group):
-        pair = step * group + offset
-        data = loose[pl.ds(pair, sources, stride=pairs), :].astype(BF16)
-        chosen = pick_cells(mm(x_table[...], data), lanes, cells_x).astype(BF16)
-        spectrum_t[offset] = mm_nt(picks[...], chosen).astype(BF16)
-        diagonal = mm(chosen, copies[...]).astype(BF16) * octets[...]
-        rows = []
-        for j in range(MX // OCT):
-            low = offset * MX * C + j * OCT * C
-            product = mm(diagonal[2 * OCT * j : 2 * OCT * (j + 1)], weights[low : low + OCT * C, :])
-            top, bottom = product[:OCT], product[OCT:]
-            rows.append(top[:, :C] - bottom[:, C:])
-            rows.append(top[:, C:] + bottom[:, :C])
-        mixed = jnp.concatenate(rows, axis=0).astype(BF16)
-        back = mm(x_back[...], mm(mixed, picks[...]).astype(BF16))
-        gathered[pl.ds(pair, 2 * wide, stride=pairs), :] = pick_cells(back, lanes, cells_x, None)
+    modes = to_modes(loose, x_table[...], source_rows[...], first, group, pairs, cells_x)
+    chosen = per_pair(modes, group, 0, rows)
+    mask = jnp.concatenate([octets[...]] * group, axis=0)
+    diagonal = mm(chosen, copies[...]).astype(BF16) * mask
+    products = []
+    for n in range(group * (MX // OCT)):
+        block = weights[n * OCT * C : (n + 1) * OCT * C, :]
+        products.append(mm(diagonal[2 * OCT * n : 2 * OCT * (n + 1)], block))
+    product = jnp.concatenate(products, axis=0).astype(BF16)
+    both = mm(product, doubled[...])
+    lanes = both.shape[1] // 2
+    mixed = []
+    for n in range(group * (MX // OCT)):
+        top = both[2 * OCT * n : 2 * OCT * n + OCT]
+        bottom = both[2 * OCT * n + OCT : 2 * OCT * (n + 1)]
+        mixed.append(top[:, :lanes] - bottom[:, lanes:])
+        mixed.append(top[:, lanes:] + bottom[:, :lanes])
+    mixed = jnp.concatenate(mixed, axis=0).astype(BF16)
+    from_modes(mixed, x_back[...], mode_rows[...], gathered, first, group, pairs, cells_x)
+    for n in range(group):
+        spectrum_t[n] = mm_nt(picks[...], chosen[n * rows : (n + 1) * rows]).astype(BF16)
 
     @pl.when(step == pl.num_programs(0) - 1)
     def _():
@@ -306,43 +327,85 @@
 
 
 def grad_kernel(
-    cells_x, wide, group, arrived, weights, spectrum_t, x_table, x_back, masks, sides, octets,
-    octets_t, shrink, out_ref, weight_grad, loose, gathered,
+    cells_x, wide, group, arrived, weights, spectrum_t, x_table, x_back, source_rows, mode_rows,
+    sides, octets, octets_t, shrink, out_ref, weight_grad, loose, gathered,
 ):
     step = pl.program_id(0)
     pairs = arrived.shape[2]
-    sources = arrived.shape[0] * 2
+    rows = 2 * MX
+    first = step * group
 
     @pl.when(step == 0)
     def _():
         unpack_pairs(arrived, loose)
 
-    lanes = masks[...]
-    for offset in range(group):
-        pair = step * group + offset
-        data = loose[pl.ds(pair, sources, stride=pairs), :].astype(BF16)
-        product = mm(x_table[...], data)
-        straight = pick_cells(product, lanes, cells_x).astype(BF16)
-        turned = pick_cells(product, lanes, cells_x, 2 * MX * cells_x).astype(BF16)
-        stacked = mm(jnp.concatenate([straight, turned], axis=1), sides[...]).astype(BF16)
-        tall = jnp.concatenate([spectrum_t[offset]] * MX, axis=0) * octets_t[...]
-        low = offset * MX * C
-        weight_grad[low : low + MX * C, :] = mm(tall, stacked)
-        rows = []
-        for j in range(MX // OCT):
-            block = weights[low + j * OCT * C : low + (j + 1) * OCT * C, :]
-            rows.append(mm_nt(stacked[2 * OCT * j : 2 * OCT * (j + 1)], block))
-        coeff = jnp.concatenate(rows, axis=0).astype(BF16) * octets[...]
-        back = mm(x_back[...], mm(coeff, shrink[...]).astype(BF16))
-        gathered[pl.ds(pair, 2 * wide, stride=pairs), :] = pick_cells(back, lanes, cells_x, None)
+    modes = to_modes(loose, x_table[...], source_rows[...], first, group, pairs, cells_x)
+    straight = per_pair(modes, group, 0, rows)
+    turned = per_pair(modes, group, rows, 2 * rows)
+    stacked = mm(jnp.concatenate([straight, turned], axis=1), sides[...]).astype(BF16)
+    coeffs = []
+    for n in range(group * (MX // OCT)):
+        block = weights[n * OCT * C : (n + 1) * OCT * C, :]
+        coeffs.append(mm_nt(stacked[2 * OCT * n : 2 * OCT * (n + 1)], block))
+    mask = jnp.concatenate([octets[...]] * group, axis=0)
+    coeff = jnp.concatenate(coeffs, axis=0).astype(BF16) * mask
+    spread = mm(coeff, shrink[...]).astype(BF16)
+    from_modes(spread, x_back[...], mode_rows[...], gathered, first, group, pairs, cells_x)
+    for n in range(group):
+        tall = jnp.concatenate([spectrum_t[n]] * MX, axis=0) * octets_t[...]
+        weight_grad[n * MX * C : (n + 1) * MX * C, :] = mm(tall, stacked[n * rows : (n + 1) * rows])
 
     @pl.when(step == pl.num_programs(0) - 1)
     def _():
         send_pairs(gathered, out_ref, wide)
 
 
-def exchange(blocks):
-    return lax.all_to_all(blocks, ("narrow", "wide"), split_axis=0, concat_axis=0, tiled=True)
+def exchange_kernel(parts, wide, sent, arrived, send_sem, recv_sem):
+    count = parts * wide
+    me = lax.axis_index("narrow") * wide + lax.axis_index("wide")
+
+    def device(place):
+        return {"narrow": lax.div(place, wide), "wide": lax.rem(place, wide)}
+
+    barrier = pltpu.get_barrier_semaphore()
+    for shift in range(1, count):
+        pl.semaphore_signal(
+            barrier,
+            inc=1,
+            device_id=device(lax.rem(me + shift, count)),
+            device_id_type=pl.DeviceIdType.MESH,
+        )
+    pl.semaphore_wait(barrier, count - 1)
+    copies = []
+    for shift in range(1, count):
+        target = lax.rem(me + shift, count)
+        copy = pltpu.make_async_remote_copy(
+            src_ref=sent.at[target],
+            dst_ref=arrived.at[me],
+            send_sem=send_sem.at[shift - 1],
+            recv_sem=recv_sem.at[shift - 1],
+            device_id=device(target),
+            device_id_type=pl.DeviceIdType.MESH,
+        )
+        copy.start()
+        copies.append(copy)
+    arrived[me] = sent[me]
+    for copy in copies:
+        copy.wait()
+
+
+def exchange(blocks, parts, wide, place):
+    return pl.pallas_call(
+        functools.partial(exchange_kernel, parts, wide),
+        out_shape=jax.ShapeDtypeStruct(blocks.shape, BF16),
+        in_specs=[pl.BlockSpec(memory_space=pltpu.VMEM)],
+        out_specs=pl.BlockSpec(memory_space=pltpu.VMEM),
+        scratch_shapes=[
+            pltpu.SemaphoreType.DMA((parts * wide - 1,)),
+            pltpu.SemaphoreType.DMA((parts * wide - 1,)),
+        ],
+        compiler_params=pltpu.CompilerParams(collective_id=place, has_side_effects=True),
+    )(blocks)
 
 
 def whole_spec(shape):
@@ -360,7 +423,7 @@
     targets = parts * wide
     pairs = spectral_weight.shape[1]
     band = 16
-    group = max(g for g in (4, 3, 2, 1) if pairs % g == 0)
+    group = max(g for g in range(1, 13) if pairs % g == 0)
     down = 1.0 / math.sqrt(depth)
     z_fwd = z_forward_table(depth, down, down)
     z_fwd_back = z_inverse_table(depth, down, down)
@@ -380,7 +443,8 @@
         )
     )
     x_dual_fwd = x_inverse_table(span_x, wide, cells_x, 1.0 / math.sqrt(span_x))
-    masks = lane_masks(cells_x)
+    source_rows = cell_mask(cells_x, 2 * targets)
+    mode_rows = cell_mask(cells_x, 2 * MX)
     lane_c = np.arange(lanes) // cells_x
     picks_np = np.arange(C)[:, None] == lane_c[None, :]
     picks = const(picks_np)
@@ -395,6 +459,10 @@
     sides_np[:lanes, :C] = picks_np.T
     sides_np[lanes:, C:] = picks_np.T
     sides = const(sides_np)
+    doubled_np = np.zeros((2 * C, 2 * lanes))
+    doubled_np[:C, :lanes] = picks_np
+    doubled_np[C:, lanes:] = picks_np
+    doubled = const(doubled_np)
     spread = const((np.arange(C * band) // band)[:, None] == np.arange(C)[None, :])
     band_index = np.arange(C * band) % band
     band_mask = const(band_index[:, None] == band_index[None, :])
@@ -419,9 +487,9 @@
         scratch_shapes=[held, turned],
         compiler_params=params,
     )(field, y_fwd, z_fwd)
-    arrived = exchange(sent)
-
-    operands = (x_fwd, x_inv, masks, copies, octets, picks)
+    arrived = exchange(sent, parts, wide, 0)
+
+    operands = (x_fwd, x_inv, source_rows, mode_rows, copies, octets, picks, doubled)
     sent, spectrum_t = pl.pallas_call(
         functools.partial(mix_kernel, cells_x, wide, group),
         grid=(pairs // group,),
@@ -431,7 +499,7 @@
         scratch_shapes=[loose, gathered],
         compiler_params=params,
     )(arrived, weights, *operands)
-    arrived = exchange(sent)
+    arrived = exchange(sent, parts, wide, 1)
 
     layer_out, slope, sent = pl.pallas_call(
         functools.partial(middle_kernel, cells_x, band),
@@ -442,9 +510,11 @@
         arrived, field, upstream, spread, channel_mixer.T, band_mask, channel_bias[:, None],
         y_inv, z_inv, y_dual_inv, z_inv_back,
     )
-    arrived = exchange(sent)
-
-    operands = (x_dual_inv, x_dual_fwd, masks, sides, octets, octets_t, shrink)
+    arrived = exchange(sent, parts, wide, 2)
+
+    operands = (
+        x_dual_inv, x_dual_fwd, source_rows, mode_rows, sides, octets, octets_t, shrink,
+    )
     sent, weight_grad = pl.pallas_call(
         functools.partial(grad_kernel, cells_x, wide, group),
         grid=(pairs // group,),
@@ -455,7 +525,7 @@
         scratch_shapes=[loose, gathered],
         compiler_params=params,
     )(arrived, weights, spectrum_t, *operands)
-    arrived = exchange(sent)
+    arrived = exchange(sent, parts, wide, 3)
 
     state_grad = pl.pallas_call(
         functools.partial(final_kernel, cells_x, band),

time: 153 us -> 133 us (0.87)
  blocking collectives: 45.5 us -> 0 us
  Pallas kernels: 86.6 us -> 109 us
  local copies, waits for them, and re-layouts: 5.46 us -> 21.5 us
  waiting for transfers between devices: 10.8 us -> 0 us
  starting transfers between devices: 3.54 us -> 0 us
    pallas_call x0 -> x4, Pallas kernels: none -> 55.7 us  [exchange(): pl.pallas_call(functools.partial(exchange_kernel, parts, wide), out_shape...]
    all_to_all x3 -> x0, blocking collectives: 45.5 us -> none  [exchange(): lax.all_to_all(blocks, ('narrow', 'wide'), split_axis=0, concat_axis=0, t...]
    pallas_call x1, Pallas kernels: 25.2 us -> 5.72 us  [body(): pl.pallas_call(functools.partial(mix_kernel, cells_x, wide, group), grid=...]
    unnamed x49 -> x75, local copies, waits for them, and re-layouts: 3.57 us -> 20.2 us
    pallas_call x1, Pallas kernels: 24.9 us -> 11.4 us  [body(): pl.pallas_call(functools.partial(grad_kernel, cells_x, wide, group), grid...]
    all_to_all x1 -> x0, waiting for transfers between devices: 10.8 us -> none  [exchange(): lax.all_to_all(blocks, ('narrow', 'wide'), split_axis=0, concat_axis=0, t...]
    all_to_all x1 -> x0, starting transfers between devices: 3.54 us -> none  [exchange(): lax.all_to_all(blocks, ('narrow', 'wide'), split_axis=0, concat_axis=0, t...]
    pallas_call x4 -> x0, local copies, waits for them, and re-layouts: 1.63 us -> none  [the longest x1 0.94 us: body(): pl.pallas_call(functools.partial(mix_kernel, cells_x, wide, group), grid=...]
  transfers between devices with their start and end apart: 1 -> 0, of which waited for: 1 -> 0; matrix products, arithmetic and copies ran while one was open for 0% -> 0% of each run, Pallas kernels for 0% -> 0%
where the time goes in v1:
time: 133 us; the launch traced here: 132 us
  Pallas kernels  109 us (82%)
  local copies, waits for them, and re-layouts  21.5 us (16%)
    pallas_call x4, Pallas kernels, exchange(): pl.pallas_call(functools.partial(exchange_kernel, parts, wide), out_shape...  55.7 us
    unnamed x75, local copies, waits for them, and re-layouts  20.2 us
    pallas_call x1, Pallas kernels, body(): pl.pallas_call(functools.partial(middle_kernel, cells_x, band), out_shape...  19.7 us
    pallas_call x1, Pallas kernels, body(): pl.pallas_call(functools.partial(grad_kernel, cells_x, wide, group), grid...  11.4 us
    pallas_call x1, Pallas kernels, body(): pl.pallas_call(functools.partial(final_kernel, cells_x, band), out_shape=...  9.59 us
    pallas_call x1, Pallas kernels, body(): pl.pallas_call(functools.partial(forward_kernel, cells_x), out_shape=mess...  7.08 us
    pallas_call x1, Pallas kernels, body(): pl.pallas_call(functools.partial(mix_kernel, cells_x, wide, group), grid=...  5.72 us

profile of v1, /device:TPU:0, one launch (start us, length us, event | category | flops | bytes accessed | tf_op | source)
XLA Modules:
  0.0 131.6 jit_solution(17148519461209232135)
XLA Ops:
  0.7 1.4 %copy.31 = bf16[32,32]{0,1:T(8,128)(2,1)} copy(bf16[32,32]{1,0:T(8,128)(2,1)} %mixer.1) | data formatting | bytes 4096 | tf_op args[2]
  2.0 1.3 %copy.32.bias = f32[32,1]{1,0:T(8,128)} copy(f32[32,1]{0,1:T(1,128)} %bitcast.15) | data formatting | bytes 256 | tf_op jit(solution)/shard_map/broadcast_in_dim | solution.py:510
  3.4 1.6 %copy-done = bf16[32,4,64,128]{3,2,1,0:T(8,128)(2,1)S(1)} copy-done((bf16[32,4,64,128]{3,2,1,0:T(8,128)(2,1)S(1)}, bf16[32,4,64,128]{3,2,1,0:T(8,128)(2,1)}, u32[]{:S(2)}) %copy-start) | copy-done | bytes 2097176
  5.0 0.9 copy-done.16
  5.9 0.8 copy-done.28
  6.8 7.1 %shard_map.283.sent = bf16[16,2,36,128]{3,2,1,0:T(8,128)(2,1)S(1)} custom-call(bf16[32,256,128]{2,1,0:T(8,128)(2,1)S(1)} %bitcast.9, bf16[2,192,256]{2,1,0:T(8,128)(2,1)S(1)} %copy-done.16, bf16[256,128]{1,0:T(8,128)(2,1)S(1)} %copy-done.28), custom_call_target="tpu_custom_call" | custom-call | tf_op jit(solution)/shard_map/pallas_call | solution.py:484
  13.9 0.7 copy-done.6
  14.6 15.3 %shard_map.284.arrived = bf16[16,2,36,128]{3,2,1,0:T(8,128)(2,1)} custom-call(bf16[16,2,36,128]{3,2,1,0:T(8,128)(2,1)} %copy-done.6), custom_call_target="tpu_custom_call" | custom-call | tf_op jit(solution)/shard_map/pallas_call | solution.py:398
  30.0 1.0 copy-done.4
  30.9 5.7 %shard_map.285 = (bf16[16,2,36,128]{3,2,1,0:T(8,128)(2,1)S(1)}, bf16[36,32,48]{2,1,0:T(8,128)(2,1)S(1)}) custom-call(bf16[16,2,36,128]{3,2,1,0:T(8,128)(2,1)S(1)} %copy-done.4, bf16[27648,64]{1,0:T(8,128)(2,1)} %bitcast.11, bf16[48,128]{1,0:T(8,128)(2,1)S(1)} %copy-done.33, bf16[16,192]{1,0:T(8,128)(2,1)S(1)} %copy-done.36, bf16[128,128]{1,0:T(8,128)(2,1)S(1)} %copy-done.17, ...), custom_call_target="tpu_custom_call" | custom-call | tf_op jit(solution)/shard_map/pallas_call | solution.py:493
  36.7 0.7 copy-done.10
  37.4 13.7 %shard_map.286.arrived = bf16[16,2,36,128]{3,2,1,0:T(8,128)(2,1)} custom-call(bf16[16,2,36,128]{3,2,1,0:T(8,128)(2,1)} %copy-done.10), custom_call_target="tpu_custom_call" | custom-call | tf_op jit(solution)/shard_map/pallas_call | solution.py:398
  51.2 1.0 copy-done.3
  52.2 0.8 copy-done.24
  53.0 0.8 copy-done.25
  53.8 0.7 copy-done.27
  54.6 0.7 copy-done.31
  55.3 19.7 %shard_map.287 = (bf16[32,256,128]{2,1,0:T(8,128)(2,1)}, bf16[32,256,128]{2,1,0:T(8,128)(2,1)S(1)}, bf16[16,2,36,128]{3,2,1,0:T(8,128)(2,1)S(1)}) custom-call(bf16[16,2,36,128]{3,2,1,0:T(8,128)(2,1)S(1)} %copy-done.3, bf16[32,256,128]{2,1,0:T(8,128)(2,1)} %bitcast.8, bf16[32,256,128]{2,1,0:T(8,128)(2,1)} %bitcast.13, bf16[512,32]{1,0:T(8,128)(2,1)S(1)} %copy-done.7, ...), custom_call_target="tpu_custom_call" | custom-call | tf_op jit(solution)/shard_map/pallas_call | solution.py:504
  74.9 0.7 copy-done.9
  75.6 13.3 %shard_map.288.arrived = bf16[16,2,36,128]{3,2,1,0:T(8,128)(2,1)} custom-call(bf16[16,2,36,128]{3,2,1,0:T(8,128)(2,1)} %copy-done.9), custom_call_target="tpu_custom_call" | custom-call | tf_op jit(solution)/shard_map/pallas_call | solution.py:398
  89.0 1.0 copy-done.2
  89.9 0.9 copy-done.15
  90.9 0.8 copy-done.18
  91.6 0.7 copy-done.20
  92.4 0.8 copy-done.22
  93.2 0.8 copy-done.23
  94.0 0.7 copy-done.32
  95.5 11.4 %shard_map.289 = (bf16[16,2,36,128]{3,2,1,0:T(8,128)(2,1)S(1)}, f32[27648,64]{1,0:T(8,128)}) custom-call(bf16[16,2,36,128]{3,2,1,0:T(8,128)(2,1)S(1)} %copy-done.2, bf16[27648,64]{1,0:T(8,128)(2,1)} %bitcast.12, bf16[36,32,48]{2,1,0:T(8,128)(2,1)S(1)} %get-tuple-element.13.spectrum_t, bf16[96,128]{1,0:T(8,128)(2,1)S(1)} %copy-done.32, ...), custom_call_target="tpu_custom_call" | custom-call | tf_op jit(solution)/shard_map/pallas_call | solution.py:518
  106.9 0.7 copy-done.8
  107.6 13.4 %shard_map.290.arrived = bf16[16,2,36,128]{3,2,1,0:T(8,128)(2,1)} custom-call(bf16[16,2,36,128]{3,2,1,0:T(8,128)(2,1)} %copy-done.8), custom_call_target="tpu_custom_call" | custom-call | tf_op jit(solution)/shard_map/pallas_call | solution.py:398
  121.0 1.0 copy-done.5
  122.0 9.6 %shard_map.291 = bf16[32,256,128]{2,1,0:T(8,128)(2,1)} custom-call(bf16[16,2,36,128]{3,2,1,0:T(8,128)(2,1)S(1)} %copy-done.5, bf16[32,256,128]{2,1,0:T(8,128)(2,1)S(1)} %get-tuple-element.15.slope, bf16[512,32]{1,0:T(8,128)(2,1)S(1)} %copy-done.7, bf16[32,32]{1,0:T(8,128)(2,1)S(1)} %copy-done.30, bf16[512,512]{1,0:T(8,128)(2,1)S(1)} %copy-done.1, ...), custom_call_target="tpu_custom_call" | custom-call | tf_op jit(solution)/shard_map/pallas_call | solution.py:530
  (53 shorter events, 0.8 us)
Async XLA Ops:
  0.6 29.2 %copy-start.19 = (bf16[48,256]{1,0:T(8,128)(2,1)S(1)}, bf16[48,256]{1,0:T(8,128)(2,1)}, u32[]{:S(2)}) copy-start(bf16[48,256]{1,0:T(8,128)(2,1)} %constant.79.octets) | copy-start | bytes 73732
  0.6 29.2 %copy-start.13 = (bf16[192,128]{1,0:T(8,128)(2,1)S(1)}, bf16[192,128]{1,0:T(8,128)(2,1)}, u32[]{:S(2)}) copy-start(bf16[192,128]{1,0:T(8,128)(2,1)} %constant.77.mode_rows) | copy-start | bytes 147460
  3.4 1.6 %copy-start = (bf16[32,4,64,128]{3,2,1,0:T(8,128)(2,1)S(1)}, bf16[32,4,64,128]{3,2,1,0:T(8,128)(2,1)}, u32[]{:S(2)}) copy-start(bf16[32,4,64,128]{3,2,1,0:T(8,128)(2,1)} %param.28) | copy-start | bytes 6291460
  5.0 0.9 copy-start.16
  5.9 0.8 copy-start.28
  6.7 23.2 %copy-start.17 = (bf16[128,128]{1,0:T(8,128)(2,1)S(1)}, bf16[128,128]{1,0:T(8,128)(2,1)}, u32[]{:S(2)}) copy-start(bf16[128,128]{1,0:T(8,128)(2,1)} %constant.76.source_rows) | copy-start | bytes 98308
  6.7 23.2 %copy-start.26 = (bf16[128,256]{1,0:T(8,128)(2,1)S(1)}, bf16[128,256]{1,0:T(8,128)(2,1)}, u32[]{:S(2)}) copy-start(bf16[128,256]{1,0:T(8,128)(2,1)} %constant.78.copies) | copy-start | bytes 196612
  6.7 23.2 %copy-start.29 = (bf16[64,256]{1,0:T(8,128)(2,1)S(1)}, bf16[64,256]{1,0:T(8,128)(2,1)}, u32[]{:S(2)}) copy-start(bf16[64,256]{1,0:T(8,128)(2,1)} %constant.81.doubled) | copy-start | bytes 98308
  6.7 23.2 %copy-start.33 = (bf16[48,128]{1,0:T(8,128)(2,1)S(1)}, bf16[48,128]{1,0:T(8,128)(2,1)}, u32[]{:S(2)}) copy-start(bf16[48,128]{1,0:T(8,128)(2,1)} %constant.74.x_table) | copy-start | bytes 36868
  6.8 23.2 %copy-start.35 = (bf16[32,128]{1,0:T(8,128)(2,1)S(1)}, bf16[32,128]{1,0:T(8,128)(2,1)}, u32[]{:S(2)}) copy-start(bf16[32,128]{1,0:T(8,128)(2,1)} %constant.80.picks) | copy-start | bytes 24580
  6.8 23.2 %copy-start.36 = (bf16[16,192]{1,0:T(8,128)(2,1)S(1)}, bf16[16,192]{1,0:T(8,128)(2,1)}, u32[]{:S(2)}) copy-start(bf16[16,192]{1,0:T(8,128)(2,1)} %constant.75.x_back) | copy-start | bytes 18436
  13.9 0.7 copy-start.6
  30.0 1.0 copy-start.4
  30.9 20.2 %copy-start.1 = (bf16[512,512]{1,0:T(8,128)(2,1)S(1)}, bf16[512,512]{1,0:T(8,128)(2,1)}, u32[]{:S(2)}) copy-start(bf16[512,512]{1,0:T(8,128)(2,1)} %constant.83.mask) | copy-start | bytes 1572868
  30.9 20.2 %copy-start.7 = (bf16[512,32]{1,0:T(8,128)(2,1)S(1)}, bf16[512,32]{1,0:T(8,128)(2,1)}, u32[]{:S(2)}) copy-start(bf16[512,32]{1,0:T(8,128)(2,1)} %constant.82.spread) | copy-start | bytes 98308
  30.9 20.2 %copy-start.11 = (bf16[2,256,192]{2,1,0:T(8,128)(2,1)S(1)}, bf16[2,256,192]{2,1,0:T(8,128)(2,1)}, u32[]{:S(2)}) copy-start(bf16[2,256,192]{2,1,0:T(8,128)(2,1)} %constant.84.y_back) | copy-start | bytes 589828
  30.9 20.2 %copy-start.14 = (bf16[2,192,256]{2,1,0:T(8,128)(2,1)S(1)}, bf16[2,192,256]{2,1,0:T(8,128)(2,1)}, u32[]{:S(2)}) copy-start(bf16[2,192,256]{2,1,0:T(8,128)(2,1)} %constant.86.y_dual) | copy-start | bytes 589828
  36.7 0.7 copy-start.10
  51.2 1.0 copy-start.3
  52.2 0.8 copy-start.24
  53.0 0.8 copy-start.25
  89.0 1.0 copy-start.2
  89.9 0.9 copy-start.15
  90.9 0.8 copy-start.18
  91.6 0.7 copy-start.20
  92.4 0.8 copy-start.22
  93.2 0.8 copy-start.23
  94.0 0.7 copy-start.32
  95.5 25.5 %copy-start.12 = (bf16[2,256,192]{2,1,0:T(8,128)(2,1)S(1)}, bf16[2,256,192]{2,1,0:T(8,128)(2,1)}, u32[]{:S(2)}) copy-start(bf16[2,256,192]{2,1,0:T(8,128)(2,1)} %constant.93.y_back) | copy-start | bytes 589828
  95.5 25.5 %copy-start.21 = (bf16[128,256]{1,0:T(8,128)(2,1)S(1)}, bf16[128,256]{1,0:T(8,128)(2,1)}, u32[]{:S(2)}) copy-start(bf16[128,256]{1,0:T(8,128)(2,1)} %constant.94.z_back) | copy-start | bytes 196612
  95.5 25.5 %copy-start.30 = (bf16[32,32]{1,0:T(8,128)(2,1)S(1)}, bf16[32,32]{1,0:T(8,128)(2,1)}, u32[]{:S(2)}) copy-start(bf16[32,32]{1,0:T(8,128)(2,1)} %mixer.1) | copy-start | bytes 6148
  121.0 1.0 copy-start.5
  (5 other events, 3.6 us)

commit v2 on v1

v2 whole, which is shorter than its diff:
```python
import functools
import math

import jax
import jax.numpy as jnp
import numpy as np
from jax import lax
from jax.experimental import pallas as pl
from jax.experimental.pallas import tpu as pltpu
from jax.sharding import PartitionSpec as P

C = 32
MX = 24
MY = 24
MZ = 24
OCT = 8
F32 = jnp.float32
BF16 = jnp.bfloat16
VMEM_LIMIT = 50 * 1024 * 1024


def mm(left, right):
    return jnp.dot(left, right, preferred_element_type=F32)


def mm_nt(left, right):
    return lax.dot_general(left, right, (((1,), (1,)), ((), ())), preferred_element_type=F32)


def const(array):
    return np.asarray(array, np.float32)


class Pack:
    def __init__(self):
        self.rows, self.places = 0, {}
        self.pieces = []

    def add(self, name, table):
        table = table.reshape((-1,) + table.shape[-2:])
        count, rows, columns = table.shape
        held = -(-rows // 16) * 16
        padded = np.zeros((count, held, 256), np.float32)
        padded[:, :rows, :columns] = table
        self.places[name] = (self.rows, held, rows, columns)
        self.pieces.append(padded.reshape(-1, 256))
        self.rows += count * held

    def array(self):
        return jnp.asarray(np.concatenate(self.pieces)).astype(BF16)

    def get(self, ref, name, part=None):
        begin, held, rows, columns = self.places[name]
        if part is None:
            return ref[begin : begin + rows, :columns]
        return ref[pl.ds(pl.multiple_of(begin + part * held, 16), rows), :columns]


def phases(points, frequency):
    turns = np.mod(frequency[:, None] * np.arange(points)[None, :], points)
    return turns.astype(np.float64) * (2.0 * math.pi / points)


def wave(points, modes, sign, scale):
    index = np.arange(modes)
    angles = phases(points, np.where(index < modes // 2, index, index - modes))
    return np.cos(angles) * scale, sign * np.sin(angles) * scale


def y_forward_table(points, parts, cells_x, scale):
    real, imag = wave(points, MY, -1.0, scale)
    local = np.stack([real, imag]).reshape(2, MY, parts, points // parts)
    table = np.einsum("sqnb,ac->nsaqcb", local, np.eye(cells_x))
    return const(table.reshape(parts, 2 * cells_x * MY, -1))


def y_inverse_table(points, parts, cells_x, scale):
    real, imag = wave(points, MY, 1.0, scale)
    local = np.stack([real, -imag]).reshape(2, MY, parts, points // parts)
    table = np.einsum("sqnb,ac->ncbsaq", local, np.eye(cells_x))
    return const(table.reshape(parts, -1, 2 * cells_x * MY))


def half_orders():
    half = np.arange(MZ // 2)
    orders = []
    for first in (0, 1):
        own = np.concatenate([half + first * MZ // 2, half + (1 - first) * MZ // 2])
        orders.append(np.concatenate([own, own + MZ, np.arange(2 * MZ, 128)]))
    return orders


def z_parts(points, first, other):
    angles = phases(points, np.arange(MZ))
    weight = np.where(np.arange(MZ) == 0, first, other)[:, None]
    return np.cos(angles) * weight, np.sin(angles) * weight


def z_forward_table(points, first, other):
    cos, sin = z_parts(points, first, other)
    table = np.zeros((2 * points, 128))
    table[:points, :MZ] = cos.T
    table[points:, :MZ] = sin.T
    table[:points, MZ : 2 * MZ] = -sin.T
    table[points:, MZ : 2 * MZ] = cos.T
    return const(np.stack([table[:, order] for order in half_orders()]))


def z_inverse_table(points, first, other):
    cos, sin = z_parts(points, first, other)
    table = np.zeros((128, 2 * points))
    table[:MZ, :points] = cos
    table[MZ : 2 * MZ, :points] = -sin
    table[:MZ, points:] = sin
    table[MZ : 2 * MZ, points:] = cos
    return const(np.stack([table[order] for order in half_orders()]))


def x_blocks(points, sign, scale):
    real, imag = wave(points, MX, sign, scale)
    table = np.stack([np.stack([real, -imag]), np.stack([imag, real])])
    return table.reshape(2, 2, MX // OCT, OCT, points)


def x_forward_table(points, wide, cells_x, scale, turned=False):
    table = x_blocks(points, -1.0, scale)
    if turned:
        table = np.stack([table[1], -table[0]])
    table = table.reshape(2, 2, MX // OCT, OCT, wide, cells_x)
    return np.einsum("rsjmwa->jrmaws", table).reshape(2 * MX, cells_x * wide * 2)


def x_inverse_table(points, wide, cells_x, scale):
    table = x_blocks(points, 1.0, scale).reshape(2, 2, MX // OCT, OCT, wide, cells_x)
    return const(np.einsum("rsjmwa->wrajsm", table).reshape(wide * 2, cells_x * 2 * MX))


def cell_mask(cells_x, rows):
    owner = np.arange(cells_x * rows) // rows
    return const(owner[:, None] == (np.arange(C * cells_x) % cells_x)[None, :])


def octet_of_rows():
    return np.arange(2 * MX) % OCT


def forward_transform(get_rows, y_table, z_table, held, turned, cells_x):
    rows = cells_x * MY
    together = 4

    def channels(step, carry):
        for offset in range(together):
            c = step * together + offset
            part = mm(y_table, get_rows(c)).astype(BF16)
            both = jnp.concatenate([part[:rows], part[rows:]], axis=1)
            held[pl.ds(pl.multiple_of(c * rows, 8), rows), :] = mm(both, z_table)
        return carry

    lax.fori_loop(0, C // together, channels, 0)
    for q in range(MY):
        block = held[pl.ds(q, C * cells_x, stride=MY), :]
        turned[pl.ds(q, 2 * MZ, stride=MY), :] = block.T[: 2 * MZ]


def inverse_transform(halves, y_table, z_table, put_rows, held, turned, cells_x):
    rows = cells_x * MY
    together = 4
    pairs = halves[0].shape[2]
    points = z_table.shape[1] // 2
    lanes = held.shape[1]
    for half, ref in enumerate(halves):
        for source in range(ref.shape[0]):
            for part in range(2):
                begin = (2 * part + half) * MZ // 2 * MY + source * pairs
                turned[begin : begin + pairs, :] = ref[source, part].astype(F32)
    for q in range(MY):
        block = turned[pl.ds(q, 2 * MZ, stride=MY), :]
        padded = jnp.concatenate([block, jnp.zeros((lanes - 2 * MZ, block.shape[1]), F32)], axis=0)
        held[pl.ds(q, C * cells_x, stride=MY), :] = padded.T

    def channels(step, carry):
        for offset in range(together):
            c = step * together + offset
            block = held[pl.ds(pl.multiple_of(c * rows, 8), rows), :].astype(BF16)
            both = mm(block, z_table).astype(BF16)
            stacked = jnp.concatenate([both[:, :points], both[:, points:]], axis=0)
            put_rows(c, mm(y_table, stacked))
        return carry

    lax.fori_loop(0, C // together, channels, 0)


def tall_mixer(spread, mixer, band, flipped):
    wide = (mm_nt if flipped else mm)(spread, mixer).astype(BF16)
    tall = mm_nt(wide, spread)
    place = lax.broadcasted_iota(jnp.int32, tall.shape, 0) % band
    same = place == lax.broadcasted_iota(jnp.int32, tall.shape, 1) % band
    return jnp.where(same, tall, 0.0).astype(BF16)


def mixed_field(table, field, begin, band):
    depth = field.shape[2]
    blocks = [field[:, pl.ds(begin + half * band, band), :] for half in range(2)]
    flat = [block.reshape(C * band, depth) for block in blocks]
    product = mm(table, jnp.concatenate(flat, axis=1))
    return [product[:, half * depth : (half + 1) * depth].reshape(C, band, depth) for half in range(2)]


def activate(band, field, upstream, table, offset, spectral, layer_out, slope):
    alpha = math.sqrt(2.0 / math.pi)
    cubic = alpha * 0.044715

    def bands(step, carry):
        begin = pl.multiple_of(step * 2 * band, 2 * band)
        linear = mixed_field(table, field, begin, band)
        for half in range(2):
            where = pl.ds(begin + half * band, band)
            v = spectral[:, where, :] + (linear[half] + offset)
            square = v * v
            t = jnp.tanh(v * (alpha + cubic * square))
            gate = 0.5 + 0.5 * t
            layer_out[:, where, :] = (v * gate).astype(BF16)
            rise = (0.5 * v) * (1.0 - t * t) * (alpha + (3.0 * cubic) * square)
            grad = upstream[:, where, :].astype(F32) * (gate + rise)
            slope[:, where, :] = grad.astype(BF16)
        return carry

    lax.fori_loop(0, field.shape[1] // (2 * band), bands, 0)


def final_kernel(pack, cells_x, band, own, other, slope, mixer, tables, out_ref, held, turned, spectral):
    me = lax.axis_index("narrow")

    def put(c, rows):
        spectral[c] = rows

    y_table, z_table = pack.get(tables, "y_back", me), pack.get(tables, "z_back", me)
    inverse_transform((own, other), y_table, z_table, put, held, turned, cells_x)
    table = tall_mixer(pack.get(tables, "spread"), mixer[...], band, False)

    def bands(step, carry):
        begin = pl.multiple_of(step * 2 * band, 2 * band)
        linear = mixed_field(table, slope, begin, band)
        for half in range(2):
            where = pl.ds(begin + half * band, band)
            out_ref[:, where, :] = (spectral[:, where, :] + linear[half]).astype(BF16)
        return carry

    lax.fori_loop(0, slope.shape[1] // (2 * band), bands, 0)


def unpack_pairs(arrived, loose):
    pairs = arrived.shape[2]
    for source in range(arrived.shape[0]):
        for part in range(2):
            begin = (source * 2 + part) * pairs
            loose[begin : begin + pairs, :] = arrived[source, part].astype(F32)


def to_modes(loose, x_table, cell_rows, first, group, pairs, cells_x):
    count = loose.shape[0] // pairs
    blocks = []
    for offset in range(group):
        data = loose[pl.ds(first + offset, count, stride=pairs), :].astype(BF16)
        blocks.append(jnp.concatenate([data] * cells_x, axis=0) * cell_rows)
    return mm(x_table, jnp.concatenate(blocks, axis=1)).astype(BF16)


def from_modes(modes, x_back, cell_rows, gathered, first, group, pairs, cells_x):
    rows = 2 * MX
    lanes = modes.shape[1]
    blocks = []
    for offset in range(group):
        data = modes[offset * rows : (offset + 1) * rows]
        blocks.append(jnp.concatenate([data] * cells_x, axis=0) * cell_rows)
    back = mm(x_back, jnp.concatenate(blocks, axis=1))
    for offset in range(group):
        where = pl.ds(first + offset, x_back.shape[0], stride=pairs)
        gathered[where, :] = back[:, offset * lanes : (offset + 1) * lanes]


def greet(wide):
    barrier = pltpu.get_barrier_semaphore()
    place, core = lax.axis_index("wide"), lax.axis_index("narrow")
    for shift in range(1, wide):
        signal(barrier, {"wide": lax.rem(place + shift, wide)})
    signal(barrier, {"narrow": 1 - core})


def signal(barrier, device):
    pl.semaphore_signal(barrier, inc=1, device_id=device, device_id_type=pl.DeviceIdType.MESH)


def met(wide):
    pl.semaphore_wait(pltpu.get_barrier_semaphore(), wide)


def remote(source, target, sems, index, device):
    return pltpu.make_async_remote_copy(
        src_ref=source,
        dst_ref=target,
        send_sem=sems[0].at[index],
        recv_sem=sems[1].at[index],
        device_id=device,
        device_id_type=pl.DeviceIdType.MESH,
    )


def start_wide(message, arrived, sems, wide):
    place = lax.axis_index("wide")
    copies = []
    for shift in range(1, wide):
        target = lax.rem(place + shift, wide)
        copy = remote(message.at[target], arrived.at[place], sems, shift, {"wide": target})
        copy.start()
        copies.append(copy)
    arrived[place] = message[place]
    return copies


def gather_modes(turned, message, arrived, mate_out, mate_in, sems, mate_sems, wide):
    half = MZ // 2 * MY
    pairs = message.shape[2]
    for part in range(2):
        begin = (2 * part + 1) * half
        mate_out[part] = turned[begin : begin + half, :].astype(BF16)
    swap = remote(mate_out, mate_in, mate_sems, 0, {"narrow": 1 - lax.axis_index("narrow")})
    swap.start()
    swap.wait()
    for part in range(2):
        total = turned[2 * part * half : (2 * part + 1) * half, :] + mate_in[part].astype(F32)
        for target in range(wide):
            begin = target * pairs
            message[target, part] = total[begin : begin + pairs].astype(BF16)
    for copy in start_wide(message, arrived, sems, wide):
        copy.wait()


def scatter_cells(gathered, message, own, other, sems, mate_sems, wide):
    pairs = message.shape[2]
    place, mate = lax.axis_index("wide"), 1 - lax.axis_index("narrow")
    for target in range(wide):
        for part in range(2):
            begin = (target * 2 + part) * pairs
            message[target, part] = gathered[begin : begin + pairs, :].astype(BF16)
    copies = start_wide(message, own, sems, wide)
    passed = [remote(own.at[place], other.at[place], mate_sems, 0, {"narrow": mate})]
    passed[0].start()
    for shift, copy in enumerate(copies, 1):
        copy.wait_recv()
        source = lax.rem(place + wide - shift, wide)
        onward = remote(own.at[source], other.at[source], mate_sems, shift, {"narrow": mate})
        onward.start()
        passed.append(onward)
    for copy in copies:
        copy.wait_send()
    for onward in passed:
        onward.wait()


def per_pair(array, group, low, high):
    lanes = array.shape[1] // group
    parts = [array[low:high, n * lanes : (n + 1) * lanes] for n in range(group)]
    return jnp.concatenate(parts, axis=0)


def weight_rows(weights, pair, j):
    begin = pl.multiple_of(pair * MX * C + j * OCT * C, OCT * C)
    return weights[pl.ds(begin, OCT * C), :]


def mix_pairs(pack, tables, cells_x, group, pairs, first, weights, loose, gathered, spectrum_t):
    rows = 2 * MX
    octets = pack.get(tables, "octets")
    picks = pack.get(tables, "picks")
    modes = to_modes(
        loose, pack.get(tables, "x"), pack.get(tables, "sources"), first, group, pairs, cells_x
    )
    chosen = per_pair(modes, group, 0, rows)
    mask = jnp.concatenate([octets] * group, axis=0)
    diagonal = mm(chosen, pack.get(tables, "copies")).astype(BF16) * mask
    products = []
    for n in range(group * (MX // OCT)):
        block = weight_rows(weights, first + n // (MX // OCT), n % (MX // OCT))
        products.append(mm(diagonal[2 * OCT * n : 2 * OCT * (n + 1)], block))
    product = jnp.concatenate(products, axis=0).astype(BF16)
    both = mm(product, pack.get(tables, "doubled"))
    lanes = both.shape[1] // 2
    mixed = []
    for n in range(group * (MX // OCT)):
        top = both[2 * OCT * n : 2 * OCT * n + OCT]
        bottom = both[2 * OCT * n + OCT : 2 * OCT * (n + 1)]
        mixed.append(top[:, :lanes] - bottom[:, lanes:])
        mixed.append(top[:, lanes:] + bottom[:, :lanes])
    mixed = jnp.concatenate(mixed, axis=0).astype(BF16)
    from_modes(
        mixed, pack.get(tables, "x_back"), pack.get(tables, "modes"), gathered, first, group,
        pairs, cells_x,
    )
    for n in range(group):
        turned = mm_nt(picks, chosen[n * rows : (n + 1) * rows])
        spectrum_t[first + n] = turned.astype(BF16)


def grad_pairs(pack, tables, cells_x, group, pairs, first, weights, loose, gathered, factors):
    rows = 2 * MX
    modes = to_modes(
        loose, pack.get(tables, "x"), pack.get(tables, "sources"), first, group, pairs, cells_x
    )
    straight = per_pair(modes, group, 0, rows)
    turned = per_pair(modes, group, rows, 2 * rows)
    both = jnp.concatenate([straight, turned], axis=1)
    stacked = mm(both, pack.get(tables, "sides")).astype(BF16)
    coeffs = []
    for n in range(group * (MX // OCT)):
        block = weight_rows(weights, first + n // (MX // OCT), n % (MX // OCT))
        coeffs.append(mm_nt(stacked[2 * OCT * n : 2 * OCT * (n + 1)], block))
    mask = jnp.concatenate([pack.get(tables, "octets")] * group, axis=0)
    coeff = jnp.concatenate(coeffs, axis=0).astype(BF16) * mask
    spread = mm(coeff, pack.get(tables, "shrink")).astype(BF16)
    from_modes(
        spread, pack.get(tables, "x_back"), pack.get(tables, "modes"), gathered, first, group,
        pairs, cells_x,
    )
    for n in range(group):
        factors[first + n] = stacked[n * rows : (n + 1) * rows]


def first_kernel(
    pack, cells_x, wide, group, field, weights_hbm, tables, own, other, spectrum_t, held, turned,
    loose, gathered, weights, message, arrived, message_back, mate_out, mate_in, load_sem, *sems,
):
    me = lax.axis_index("narrow")
    pairs = message.shape[2]
    greet(wide)
    load = pltpu.make_async_copy(weights_hbm, weights, load_sem)
    load.start()
    y_table, z_table = pack.get(tables, "y", me), pack.get(tables, "z", me)
    forward_transform(lambda c: field[c], y_table, z_table, held, turned, cells_x)
    met(wide)
    gather_modes(turned, message, arrived, mate_out, mate_in, sems[0:2], sems[2:4], wide)
    unpack_pairs(arrived, loose)
    load.wait()

    def groups(step, carry):
        mix_pairs(
            pack, tables, cells_x, group, pairs, step * group, weights, loose, gathered, spectrum_t
        )
        return carry

    lax.fori_loop(0, pairs // group, groups, 0)
    scatter_cells(gathered, message_back, own, other, sems[4:6], sems[6:8], wide)


def second_kernel(
    pack, cells_x, wide, group, band, own_in, other_in, field, upstream, weights_hbm, mixer, bias,
    tables, layer_out, slope, own, other, factors, held, turned, loose, gathered, weights, message,
    arrived, message_back, mate_out, mate_in, load_sem, spectral, *sems,
):
    me = lax.axis_index("narrow")
    pairs = message.shape[2]
    greet(wide)
    load = pltpu.make_async_copy(weights_hbm, weights, load_sem)
    load.start()

    def put(c, rows):
        spectral[c] = rows

    y_table, z_table = pack.get(tables, "y_back", me), pack.get(tables, "z_back", me)
    inverse_transform((own_in, other_in), y_table, z_table, put, held, turned, cells_x)
    table = tall_mixer(pack.get(tables, "spread"), mixer[...], band, True)
    unit = lax.broadcasted_iota(jnp.int32, (C, C), 0) == lax.broadcasted_iota(jnp.int32, (C, C), 1)
    offset = jnp.sum(jnp.where(unit, bias[...], 0.0), axis=1, keepdims=True)[:, :, None]
    activate(band, field, upstream, table, offset, spectral, layer_out, slope)
    y_table, z_table = pack.get(tables, "y", me), pack.get(tables, "z", me)
    forward_transform(lambda c: slope[c], y_table, z_table, held, turned, cells_x)
    met(wide)
    gather_modes(turned, message, arrived, mate_out, mate_in, sems[0:2], sems[2:4], wide)
    unpack_pairs(arrived, loose)
    load.wait()

    def groups(step, carry):
        grad_pairs(
            pack, tables, cells_x, group, pairs, step * group, weights, loose, gathered, factors
        )
        return carry

    lax.fori_loop(0, pairs // group, groups, 0)
    scatter_cells(gathered, message_back, own, other, sems[4:6], sems[6:8], wide)


def weight_kernel(pack, group, spectrum_t, factors, tables, weight_grad):
    for n in range(group):
        tall = jnp.concatenate([spectrum_t[n]] * MX, axis=0) * pack.get(tables, "octets_t")
        weight_grad[n * MX * C : (n + 1) * MX * C, :] = mm(tall, factors[n])


def whole_spec(shape):
    return pl.BlockSpec(shape, lambda *_: (0,) * len(shape))


def body(plume_state, spectral_weight, channel_mixer, channel_bias, upstream_grad):
    row_count, cells_x, cells_y, depth = plume_state.shape
    wide = lax.axis_size("wide")
    parts = lax.axis_size("narrow")
    span_x = cells_x * wide
    span_y = cells_y * parts
    flat = cells_x * cells_y
    lanes = C * cells_x
    pairs = spectral_weight.shape[1]
    band = 16
    group = max(g for g in range(1, 13) if pairs % g == 0)
    strip = max(g for g in range(1, 7) if pairs % g == 0)
    down = 1.0 / math.sqrt(depth)
    z_fwd = z_forward_table(depth, down, down)
    z_fwd_back = z_inverse_table(depth, down, down)
    first, other = 1.0 / math.sqrt(2 * MZ), 2.0 / math.sqrt(2 * MZ)
    z_inv = z_inverse_table(depth, first, other)
    z_inv_back = z_forward_table(depth, first, other)
    y_fwd = y_forward_table(span_y, parts, cells_x, 1.0 / math.sqrt(span_y))
    y_inv = y_inverse_table(span_y, parts, cells_x, 1.0 / math.sqrt(MY))
    y_dual_inv = y_forward_table(span_y, parts, cells_x, 1.0 / math.sqrt(MY))
    y_dual_fwd = y_inverse_table(span_y, parts, cells_x, 1.0 / math.sqrt(span_y))
    x_fwd = const(x_forward_table(span_x, wide, cells_x, 1.0 / math.sqrt(span_x)))
    x_inv = x_inverse_table(span_x, wide, cells_x, 1.0 / math.sqrt(MX))
    scale = 1.0 / math.sqrt(MX)
    x_dual_inv = const(
        np.concatenate(
            [x_forward_table(span_x, wide, cells_x, scale, turn) for turn in (False, True)]
        )
    )
    x_dual_fwd = x_inverse_table(span_x, wide, cells_x, 1.0 / math.sqrt(span_x))
    source_rows = cell_mask(cells_x, 2 * wide)
    mode_rows = cell_mask(cells_x, 2 * MX)
    lane_c = np.arange(lanes) // cells_x
    picks_np = np.arange(C)[:, None] == lane_c[None, :]
    picks = const(picks_np)
    copies_np = np.tile(picks_np.T, (1, OCT))
    copies = const(copies_np)
    shrink = const(copies_np.T)
    octets_np = octet_of_rows()[:, None] == (np.arange(OCT * C) // C)[None, :]
    octets = const(octets_np)
    row_mode = (np.arange(2 * MX) // (2 * OCT)) * OCT + np.arange(2 * MX) % OCT
    octets_t = const((np.arange(MX * C) // C)[:, None] == row_mode[None, :])
    sides_np = np.zeros((2 * lanes, 2 * C))
    sides_np[:lanes, :C] = picks_np.T
    sides_np[lanes:, C:] = picks_np.T
    sides = const(sides_np)
    doubled_np = np.zeros((2 * C, 2 * lanes))
    doubled_np[:C, :lanes] = picks_np
    doubled_np[C:, lanes:] = picks_np
    doubled = const(doubled_np)
    spread = const((np.arange(C * band) // band)[:, None] == np.arange(C)[None, :])

    params = pltpu.CompilerParams(vmem_limit_bytes=VMEM_LIMIT)
    shape = (wide, 2, pairs, lanes)
    message = jax.ShapeDtypeStruct(shape, BF16)
    held = pltpu.VMEM((lanes * MY, 128), F32)
    turned = pltpu.VMEM((2 * MZ * MY, lanes), F32)
    spectral = pltpu.VMEM((C, flat, depth), F32)
    field = plume_state.reshape(C, flat, depth)
    upstream = upstream_grad.reshape(C, flat, depth)
    weights = spectral_weight.reshape(pairs * MX * C, 2 * C)
    field_shape = jax.ShapeDtypeStruct((C, flat, depth), BF16)
    local = pl.BlockSpec(memory_space=pltpu.VMEM)
    far = pl.BlockSpec(memory_space=pl.ANY)
    mate = pltpu.VMEM((2, MZ // 2 * MY, lanes), BF16)
    work = [
        held,
        turned,
        pltpu.VMEM((wide * 2 * pairs, lanes), F32),
        pltpu.VMEM((2 * wide * pairs, lanes), F32),
        pltpu.VMEM(weights.shape, BF16),
        pltpu.VMEM(shape, BF16),
        pltpu.VMEM(shape, BF16),
        pltpu.VMEM(shape, BF16),
        mate,
        mate,
        pltpu.SemaphoreType.DMA,
    ]
    sems = [pltpu.SemaphoreType.DMA((count,)) for count in (wide, wide, 1, 1) + (wide,) * 4]

    pack = Pack()
    pack.add("y", y_fwd)
    pack.add("z", z_fwd)
    for name, table in (
        ("x", x_fwd), ("x_back", x_inv), ("sources", source_rows), ("modes", mode_rows),
        ("copies", copies), ("octets", octets), ("picks", picks), ("doubled", doubled),
    ):
        pack.add(name, table)
    own, other, spectrum_t = pl.pallas_call(
        functools.partial(first_kernel, pack, cells_x, wide, group),
        in_specs=[local, far, local],
        out_specs=[local] * 3,
        out_shape=[message, message, jax.ShapeDtypeStruct((pairs, C, 2 * MX), BF16)],
        scratch_shapes=work + sems,
        compiler_params=pltpu.CompilerParams(
            vmem_limit_bytes=VMEM_LIMIT, collective_id=0, has_side_effects=True
        ),
    )(field, weights, pack.array())

    pack = Pack()
    pack.add("y", y_dual_inv)
    pack.add("z", z_inv_back)
    pack.add("y_back", y_inv)
    pack.add("z_back", z_inv)
    for name, table in (
        ("x", x_dual_inv), ("x_back", x_dual_fwd), ("sources", source_rows), ("modes", mode_rows),
        ("sides", sides), ("octets", octets), ("shrink", shrink), ("spread", spread),
    ):
        pack.add(name, table)
    layer_out, slope, own, other, factors = pl.pallas_call(
        functools.partial(second_kernel, pack, cells_x, wide, group, band),
        in_specs=[local] * 4 + [far] + [local] * 3,
        out_specs=[local] * 5,
        out_shape=[
            field_shape, field_shape, message, message,
            jax.ShapeDtypeStruct((pairs, 2 * MX, 2 * C), BF16),
        ],
        scratch_shapes=work + [spectral] + sems,
        compiler_params=pltpu.CompilerParams(
            vmem_limit_bytes=VMEM_LIMIT, collective_id=1, has_side_effects=True
        ),
    )(own, other, field, upstream, weights, channel_mixer, channel_bias[None, :], pack.array())

    pack = Pack()
    pack.add("octets_t", octets_t)
    tables = pack.array()
    weight_grad = pl.pallas_call(
        functools.partial(weight_kernel, pack, strip),
        grid=(pairs // (strip),),
        in_specs=[
            pl.BlockSpec((strip, C, 2 * MX), lambda i: (i, 0, 0)),
            pl.BlockSpec((strip, 2 * MX, 2 * C), lambda i: (i, 0, 0)),
            whole_spec(tables.shape),
        ],
        out_specs=pl.BlockSpec(((strip) * MX * C, 2 * C), lambda i: (i, 0)),
        out_shape=jax.ShapeDtypeStruct(weights.shape, F32),
        compiler_params=params,
    )(spectrum_t, factors, tables)

    pack = Pack()
    pack.add("y_back", y_dual_fwd)
    pack.add("z_back", z_fwd_back)
    pack.add("spread", spread)
    state_grad = pl.pallas_call(
        functools.partial(final_kernel, pack, cells_x, band),
        out_shape=field_shape,
        scratch_shapes=[held, turned, spectral],
        compiler_params=params,
    )(own, other, slope, channel_mixer, pack.array())
    return (
        layer_out.reshape(plume_state.shape),
        state_grad.reshape(plume_state.shape),
        weight_grad.reshape(spectral_weight.shape),
    )


def solution(mesh):
    in_specs = (
        P("groups", "wide", "narrow", None),
        P("narrow", "wide", None, None, None),
        P(),
        P(),
        P("groups", "wide", "narrow", None),
    )
    out_specs = (
        P("groups", "wide", "narrow", None),
        P("groups", "wide", "narrow", None),
        P("narrow", "wide", "groups", None, None),
    )
    return jax.shard_map(body, mesh=mesh, in_specs=in_specs, out_specs=out_specs, check_vma=False)
```

time: 133 us -> 88.6 us (0.67)
  Pallas kernels: 109 us -> 82 us
  local copies, waits for them, and re-layouts: 21.5 us -> 5.64 us
    pallas_call x9 -> x4, Pallas kernels: 109 us -> 82 us  [the longest x1 39.5 us: body(): pl.pallas_call(functools.partial(second_kernel, pack, cells_x, wide, grou...]
    unnamed x75 -> x19, local copies, waits for them, and re-layouts: 20.2 us -> 5.64 us
    broadcast_in_dim x1 -> x0, local copies, waits for them, and re-layouts: 1.34 us -> none  [body(): channel_bias[:, None]]
where the time goes in v2:
time: 88.6 us; the launch traced here: 88.4 us
  Pallas kernels  82 us (93%)
  local copies, waits for them, and re-layouts  5.64 us (6%)
    pallas_call x1, Pallas kernels, body(): pl.pallas_call(functools.partial(second_kernel, pack, cells_x, wide, grou...  39.5 us
    pallas_call x1, Pallas kernels, body(): pl.pallas_call(functools.partial(first_kernel, pack, cells_x, wide, group...  26.6 us
    pallas_call x1, Pallas kernels, body(): pl.pallas_call(functools.partial(final_kernel, pack, cells_x, band), out_...  9.65 us
    pallas_call x1, Pallas kernels, body(): pl.pallas_call(functools.partial(weight_kernel, pack, strip), grid=(pairs...  6.34 us
    unnamed x19, local copies, waits for them, and re-layouts  5.64 us

profile of v2, /device:TPU:0, one launch (start us, length us, event | category | flops | bytes accessed | tf_op | source)
XLA Modules:
  0.0 88.4 jit_solution(4388496155181866966)
XLA Ops:
  0.6 0.0 copy-start
  0.6 1.6 %copy-done = bf16[32,4,64,128]{3,2,1,0:T(8,128)(2,1)S(1)} copy-done((bf16[32,4,64,128]{3,2,1,0:T(8,128)(2,1)S(1)}, bf16[32,4,64,128]{3,2,1,0:T(8,128)(2,1)}, u32[]{:S(2)}) %copy-start) | copy-done | bytes 2097176
  2.2 0.0 copy-start.3
  2.2 1.1 %copy-done.3 = bf16[1488,256]{1,0:T(8,128)(2,1)S(1)} copy-done((bf16[1488,256]{1,0:T(8,128)(2,1)S(1)}, bf16[1488,256]{1,0:T(8,128)(2,1)}, u32[]{:S(2)}) %copy-start.3) | copy-done | bytes 761880
  3.4 0.0 copy-start.2
  3.4 0.0 copy-start.6
  3.4 0.0 copy-start.7
  3.4 26.6 %shard_map.112 = (bf16[8,2,36,128]{3,2,1,0:T(8,128)(2,1)S(1)}, bf16[8,2,36,128]{3,2,1,0:T(8,128)(2,1)S(1)}, bf16[36,32,48]{2,1,0:T(8,128)(2,1)S(1)}) custom-call(bf16[32,256,128]{2,1,0:T(8,128)(2,1)S(1)} %bitcast.8, bf16[27648,64]{1,0:T(8,128)(2,1)} %bitcast.10, bf16[1488,256]{1,0:T(8,128)(2,1)S(1)} %copy-done.3), custom_call_target="tpu_custom_call" | custom-call | tf_op jit(solution)/shard_map/pallas_call | solution.py:591
  30.0 0.0 copy-done.2
  30.0 0.0 copy-done.6
  30.0 0.0 copy-done.7
  30.0 0.0 copy-start.4
  30.0 39.5 %shard_map.113 = (bf16[32,256,128]{2,1,0:T(8,128)(2,1)}, bf16[32,256,128]{2,1,0:T(8,128)(2,1)}, bf16[8,2,36,128]{3,2,1,0:T(8,128)(2,1)S(1)}, bf16[8,2,36,128]{3,2,1,0:T(8,128)(2,1)S(1)}, bf16[36,48,64]{2,1,0:T(8,128)(2,1)S(1)}) custom-call(bf16[8,2,36,128]{3,2,1,0:T(8,128)(2,1)S(1)} %get-tuple-element.11.own_in, ...), custom_call_target="tpu_custom_call" | custom-call | tf_op jit(solution)/shard_map/pallas_call | solution.py:612
  69.5 0.0 copy-done.4
  69.5 0.0 copy-start.1
  69.5 1.6 %copy-done.1 = bf16[32,256,128]{2,1,0:T(8,128)(2,1)S(1)} copy-done((bf16[32,256,128]{2,1,0:T(8,128)(2,1)S(1)}, bf16[32,256,128]{2,1,0:T(8,128)(2,1)}, u32[]{:S(2)}) %copy-start.1) | copy-done | bytes 2097176
  71.1 0.0 copy-start.5
  71.1 9.6 %shard_map.114 = bf16[32,256,128]{2,1,0:T(8,128)(2,1)} custom-call(bf16[8,2,36,128]{3,2,1,0:T(8,128)(2,1)S(1)} %get-tuple-element.14.own, bf16[8,2,36,128]{3,2,1,0:T(8,128)(2,1)S(1)} %get-tuple-element.15.other, bf16[32,256,128]{2,1,0:T(8,128)(2,1)S(1)} %copy-done.1, bf16[32,32]{1,0:T(8,128)(2,1)S(1)} %copy-done.6, bf16[1280,256]{1,0:T(8,128)(2,1)S(1)} %copy-done.4), custom_call_target="tpu_custom_call" | custom-call | tf_op jit(solution)/shard_map/pallas_call | solution.py:646
  80.7 0.0 copy-done.5
  80.7 0.0 copy-start.8
  80.7 6.3 %shard_map.115 = f32[27648,64]{1,0:T(8,128)} custom-call(bf16[36,32,48]{2,1,0:T(8,128)(2,1)S(1)} %get-tuple-element.17.spectrum_t, bf16[36,48,64]{2,1,0:T(8,128)(2,1)S(1)} %get-tuple-element.18.factors, bf16[768,256]{1,0:T(8,128)(2,1)S(1)} %copy-done.5), custom_call_target="tpu_custom_call" | custom-call | tf_op jit(solution)/shard_map/pallas_call | solution.py:629
  87.1 0.0 copy-done.8
  87.1 1.3 %copy.13 = bf16[32,4,64,128]{3,2,1,0:T(8,128)(2,1)} copy(bf16[32,4,64,128]{3,2,1,0:T(8,128)(2,1)S(1)} %bitcast.14) | data formatting | bytes 4194304
Async XLA Ops:
  0.6 1.6 %copy-start = (bf16[32,4,64,128]{3,2,1,0:T(8,128)(2,1)S(1)}, bf16[32,4,64,128]{3,2,1,0:T(8,128)(2,1)}, u32[]{:S(2)}) copy-start(bf16[32,4,64,128]{3,2,1,0:T(8,128)(2,1)} %param.9) | copy-start | bytes 6291460
  2.2 1.1 %copy-start.3 = (bf16[1488,256]{1,0:T(8,128)(2,1)S(1)}, bf16[1488,256]{1,0:T(8,128)(2,1)}, u32[]{:S(2)}) copy-start(bf16[1488,256]{1,0:T(8,128)(2,1)} %constant.15.tables) | copy-start | bytes 2285572
  3.4 26.6 %copy-start.2 = (bf16[3104,256]{1,0:T(8,128)(2,1)S(1)}, bf16[3104,256]{1,0:T(8,128)(2,1)}, u32[]{:S(2)}) copy-start(bf16[3104,256]{1,0:T(8,128)(2,1)} %constant.16.tables) | copy-start | bytes 4767748
  3.4 26.6 %copy-start.6 = (bf16[32,32]{1,0:T(8,128)(2,1)S(1)}, bf16[32,32]{1,0:T(8,128)(2,1)}, u32[]{:S(2)}) copy-start(bf16[32,32]{1,0:T(8,128)(2,1)} %mixer.3) | copy-start | bytes 6148
  3.4 26.6 %copy-start.7 = (f32[32]{0:T(128)S(1)}, f32[32]{0:T(128)}, u32[]{:S(2)}) copy-start(f32[32]{0:T(128)} %param.12) | copy-start | bytes 388
  30.0 39.5 %copy-start.4 = (bf16[1280,256]{1,0:T(8,128)(2,1)S(1)}, bf16[1280,256]{1,0:T(8,128)(2,1)}, u32[]{:S(2)}) copy-start(bf16[1280,256]{1,0:T(8,128)(2,1)} %constant.17.tables) | copy-start | bytes 1966084
  69.5 1.6 %copy-start.1 = (bf16[32,256,128]{2,1,0:T(8,128)(2,1)S(1)}, bf16[32,256,128]{2,1,0:T(8,128)(2,1)}, u32[]{:S(2)}) copy-start(bf16[32,256,128]{2,1,0:T(8,128)(2,1)} %get-tuple-element.16.slope) | copy-start | bytes 6291460
  71.1 9.7 %copy-start.5 = (bf16[768,256]{1,0:T(8,128)(2,1)S(1)}, bf16[768,256]{1,0:T(8,128)(2,1)}, u32[]{:S(2)}) copy-start(bf16[768,256]{1,0:T(8,128)(2,1)} %constant.18.tables) | copy-start | bytes 1179652
  80.7 6.3 %copy-start.8 = (bf16[32,256,128]{2,1,0:T(8,128)(2,1)S(1)}, bf16[32,256,128]{2,1,0:T(8,128)(2,1)}, u32[]{:S(2)}) copy-start(bf16[32,256,128]{2,1,0:T(8,128)(2,1)} %get-tuple-element.13) | copy-start | bytes 6291460

commit v3 on v2

--- a/solution.py
+++ b/solution.py
@@ -146,7 +146,7 @@
 
 def forward_transform(get_rows, y_table, z_table, held, turned, cells_x):
     rows = cells_x * MY
-    together = 4
+    together = 16
 
     def channels(step, carry):
         for offset in range(together):
@@ -164,7 +164,7 @@
 
 def inverse_transform(halves, y_table, z_table, put_rows, held, turned, cells_x):
     rows = cells_x * MY
-    together = 4
+    together = 16
     pairs = halves[0].shape[2]
     points = z_table.shape[1] // 2
     lanes = held.shape[1]
@@ -228,25 +228,25 @@
     lax.fori_loop(0, field.shape[1] // (2 * band), bands, 0)
 
 
-def final_kernel(pack, cells_x, band, own, other, slope, mixer, tables, out_ref, held, turned, spectral):
-    me = lax.axis_index("narrow")
-
-    def put(c, rows):
-        spectral[c] = rows
-
-    y_table, z_table = pack.get(tables, "y_back", me), pack.get(tables, "z_back", me)
-    inverse_transform((own, other), y_table, z_table, put, held, turned, cells_x)
-    table = tall_mixer(pack.get(tables, "spread"), mixer[...], band, False)
-
+def mix_gradient(band, slope, table, mixed_grad):
     def bands(step, carry):
         begin = pl.multiple_of(step * 2 * band, 2 * band)
         linear = mixed_field(table, slope, begin, band)
         for half in range(2):
-            where = pl.ds(begin + half * band, band)
-            out_ref[:, where, :] = (spectral[:, where, :] + linear[half]).astype(BF16)
+            mixed_grad[:, pl.ds(begin + half * band, band), :] = linear[half].astype(BF16)
         return carry
 
     lax.fori_loop(0, slope.shape[1] // (2 * band), bands, 0)
+
+
+def final_kernel(pack, cells_x, own, other, mixed_grad, tables, out_ref, held, turned):
+    me = lax.axis_index("narrow")
+
+    def put(c, rows):
+        out_ref[c] = (rows + mixed_grad[c].astype(F32)).astype(BF16)
+
+    y_table, z_table = pack.get(tables, "y_back", me), pack.get(tables, "z_back", me)
+    inverse_transform((own, other), y_table, z_table, put, held, turned, cells_x)
 
 
 def unpack_pairs(arrived, loose):
@@ -318,7 +318,9 @@
     return copies
 
 
-def gather_modes(turned, message, arrived, mate_out, mate_in, sems, mate_sems, wide):
+def gather_modes(
+    turned, message, arrived, mate_out, mate_in, sems, mate_sems, wide, meanwhile=None
+):
     half = MZ // 2 * MY
     pairs = message.shape[2]
     for part in range(2):
@@ -332,7 +334,10 @@
         for target in range(wide):
             begin = target * pairs
             message[target, part] = total[begin : begin + pairs].astype(BF16)
-    for copy in start_wide(message, arrived, sems, wide):
+    copies = start_wide(message, arrived, sems, wide)
+    if meanwhile is not None:
+        meanwhile()
+    for copy in copies:
         copy.wait()
 
 
@@ -454,8 +459,8 @@
 
 def second_kernel(
     pack, cells_x, wide, group, band, own_in, other_in, field, upstream, weights_hbm, mixer, bias,
-    tables, layer_out, slope, own, other, factors, held, turned, loose, gathered, weights, message,
-    arrived, message_back, mate_out, mate_in, load_sem, spectral, *sems,
+    tables, layer_out, mixed_grad, own, other, factors, held, turned, loose, gathered, weights, message,
+    arrived, message_back, mate_out, mate_in, load_sem, spectral, slope, *sems,
 ):
     me = lax.axis_index("narrow")
     pairs = message.shape[2]
@@ -475,7 +480,14 @@
     y_table, z_table = pack.get(tables, "y", me), pack.get(tables, "z", me)
     forward_transform(lambda c: slope[c], y_table, z_table, held, turned, cells_x)
     met(wide)
-    gather_modes(turned, message, arrived, mate_out, mate_in, sems[0:2], sems[2:4], wide)
+
+    def meanwhile():
+        back = tall_mixer(pack.get(tables, "spread"), mixer[...], band, False)
+        mix_gradient(band, slope, back, mixed_grad)
+
+    gather_modes(
+        turned, message, arrived, mate_out, mate_in, sems[0:2], sems[2:4], wide, meanwhile
+    )
     unpack_pairs(arrived, loose)
     load.wait()
 
@@ -609,7 +621,7 @@
         ("sides", sides), ("octets", octets), ("shrink", shrink), ("spread", spread),
     ):
         pack.add(name, table)
-    layer_out, slope, own, other, factors = pl.pallas_call(
+    layer_out, mixed_grad, own, other, factors = pl.pallas_call(
         functools.partial(second_kernel, pack, cells_x, wide, group, band),
         in_specs=[local] * 4 + [far] + [local] * 3,
         out_specs=[local] * 5,
@@ -617,7 +629,7 @@
             field_shape, field_shape, message, message,
             jax.ShapeDtypeStruct((pairs, 2 * MX, 2 * C), BF16),
         ],
-        scratch_shapes=work + [spectral] + sems,
+        scratch_shapes=work + [spectral, pltpu.VMEM((C, flat, depth), BF16)] + sems,
         compiler_params=pltpu.CompilerParams(
             vmem_limit_bytes=VMEM_LIMIT, collective_id=1, has_side_effects=True
         ),
@@ -639,16 +651,16 @@
         compiler_params=params,
     )(spectrum_t, factors, tables)
 
+    own, weight_grad = lax.optimization_barrier((own, weight_grad))
     pack = Pack()
     pack.add("y_back", y_dual_fwd)
     pack.add("z_back", z_fwd_back)
-    pack.add("spread", spread)
     state_grad = pl.pallas_call(
-        functools.partial(final_kernel, pack, cells_x, band),
+        functools.partial(final_kernel, pack, cells_x),
         out_shape=field_shape,
-        scratch_shapes=[held, turned, spectral],
+        scratch_shapes=[held, turned],
         compiler_params=params,
-    )(own, other, slope, channel_mixer, pack.array())
+    )(own, other, mixed_grad, pack.array())
     return (
         layer_out.reshape(plume_state.shape),
         state_grad.reshape(plume_state.shape),

time: 88.6 us -> 80.9 us (0.913)
  Pallas kernels: 82 us -> 76 us
  local copies, waits for them, and re-layouts: 5.64 us -> 4.06 us
    pallas_call x1, Pallas kernels: 9.65 us -> 5.86 us  [body(): pl.pallas_call(functools.partial(final_kernel, pack, cells_x), out_shape=...]
    unnamed x19, local copies, waits for them, and re-layouts: 5.64 us -> 4.06 us
    pallas_call x1, Pallas kernels: 39.5 us -> 38 us  [body(): pl.pallas_call(functools.partial(second_kernel, pack, cells_x, wide, grou...]
where the time goes in v3:
time: 80.9 us; the launch traced here: 80.7 us
  Pallas kernels  76 us (94%)
  local copies, waits for them, and re-layouts  4.06 us (5%)
    pallas_call x1, Pallas kernels, body(): pl.pallas_call(functools.partial(second_kernel, pack, cells_x, wide, grou...  38 us
    pallas_call x1, Pallas kernels, body(): pl.pallas_call(functools.partial(first_kernel, pack, cells_x, wide, group...  25.8 us
    pallas_call x1, Pallas kernels, body(): pl.pallas_call(functools.partial(weight_kernel, pack, strip), grid=(pairs...  6.34 us
    pallas_call x1, Pallas kernels, body(): pl.pallas_call(functools.partial(final_kernel, pack, cells_x), out_shape=...  5.86 us
    unnamed x19, local copies, waits for them, and re-layouts  4.06 us

profile of v3, /device:TPU:0, one launch (start us, length us, event | category | flops | bytes accessed | tf_op | source)
XLA Modules:
  0.0 80.7 jit_solution(17960271712534577672)
XLA Ops:
  0.6 0.0 copy-start
  0.6 1.6 %copy-done = bf16[32,4,64,128]{3,2,1,0:T(8,128)(2,1)S(1)} copy-done((bf16[32,4,64,128]{3,2,1,0:T(8,128)(2,1)S(1)}, bf16[32,4,64,128]{3,2,1,0:T(8,128)(2,1)}, u32[]{:S(2)}) %copy-start) | copy-done | bytes 2097176
  2.2 0.0 copy-start.3
  2.2 1.1 %copy-done.3 = bf16[1488,256]{1,0:T(8,128)(2,1)S(1)} copy-done((bf16[1488,256]{1,0:T(8,128)(2,1)S(1)}, bf16[1488,256]{1,0:T(8,128)(2,1)}, u32[]{:S(2)}) %copy-start.3) | copy-done | bytes 761880
  3.4 0.0 copy-start.2
  3.4 0.0 copy-start.6
  3.4 0.0 copy-start.7
  3.4 25.8 %shard_map.112 = (bf16[8,2,36,128]{3,2,1,0:T(8,128)(2,1)S(1)}, bf16[8,2,36,128]{3,2,1,0:T(8,128)(2,1)S(1)}, bf16[36,32,48]{2,1,0:T(8,128)(2,1)S(1)}) custom-call(bf16[32,256,128]{2,1,0:T(8,128)(2,1)S(1)} %bitcast.8, bf16[27648,64]{1,0:T(8,128)(2,1)} %bitcast.10, bf16[1488,256]{1,0:T(8,128)(2,1)S(1)} %copy-done.3), custom_call_target="tpu_custom_call" | custom-call | tf_op jit(solution)/shard_map/pallas_call | solution.py:603
  29.1 0.0 copy-done.2
  29.2 0.0 copy-done.6
  29.2 0.0 copy-done.7
  29.2 0.0 copy-start.5
  29.2 38.0 %shard_map.113 = (bf16[32,256,128]{2,1,0:T(8,128)(2,1)}, bf16[32,256,128]{2,1,0:T(8,128)(2,1)}, bf16[8,2,36,128]{3,2,1,0:T(8,128)(2,1)S(1)}, bf16[8,2,36,128]{3,2,1,0:T(8,128)(2,1)S(1)}, bf16[36,48,64]{2,1,0:T(8,128)(2,1)S(1)}) custom-call(bf16[8,2,36,128]{3,2,1,0:T(8,128)(2,1)S(1)} %get-tuple-element.13.own_in, ...), custom_call_target="tpu_custom_call" | custom-call | tf_op jit(solution)/shard_map/pallas_call | solution.py:624
  67.2 0.0 copy-done.5
  67.2 0.0 copy-start.1
  67.2 0.0 copy-start.4
  67.2 6.3 %shard_map.114 = f32[27648,64]{1,0:T(8,128)} custom-call(bf16[36,32,48]{2,1,0:T(8,128)(2,1)S(1)} %get-tuple-element.17.spectrum_t, bf16[36,48,64]{2,1,0:T(8,128)(2,1)S(1)} %get-tuple-element.18.factors, bf16[768,256]{1,0:T(8,128)(2,1)S(1)} %copy-done.5), custom_call_target="tpu_custom_call" | custom-call | tf_op jit(solution)/shard_map/pallas_call | solution.py:641
  73.5 0.0 copy-done.1
  73.5 0.0 copy-done.4
  73.5 0.0 copy-start.8
  73.5 5.9 %shard_map.115 = bf16[32,256,128]{2,1,0:T(8,128)(2,1)} custom-call(bf16[8,2,36,128]{3,2,1,0:T(8,128)(2,1)S(1)} %get-tuple-element.19.own, bf16[8,2,36,128]{3,2,1,0:T(8,128)(2,1)S(1)} %get-tuple-element.20.other, bf16[32,256,128]{2,1,0:T(8,128)(2,1)S(1)} %copy-done.1, bf16[768,256]{1,0:T(8,128)(2,1)S(1)} %copy-done.4), custom_call_target="tpu_custom_call" | custom-call | tf_op jit(solution)/shard_map/pallas_call | solution.py:658
  79.4 0.0 copy-done.8
  79.4 1.3 %copy.13 = bf16[32,4,64,128]{3,2,1,0:T(8,128)(2,1)} copy(bf16[32,4,64,128]{3,2,1,0:T(8,128)(2,1)S(1)} %bitcast.14) | data formatting | bytes 4194304
Async XLA Ops:
  0.6 1.6 %copy-start = (bf16[32,4,64,128]{3,2,1,0:T(8,128)(2,1)S(1)}, bf16[32,4,64,128]{3,2,1,0:T(8,128)(2,1)}, u32[]{:S(2)}) copy-start(bf16[32,4,64,128]{3,2,1,0:T(8,128)(2,1)} %param.9) | copy-start | bytes 6291460
  2.2 1.1 %copy-start.3 = (bf16[1488,256]{1,0:T(8,128)(2,1)S(1)}, bf16[1488,256]{1,0:T(8,128)(2,1)}, u32[]{:S(2)}) copy-start(bf16[1488,256]{1,0:T(8,128)(2,1)} %constant.15.tables) | copy-start | bytes 2285572
  3.4 25.8 %copy-start.2 = (bf16[3104,256]{1,0:T(8,128)(2,1)S(1)}, bf16[3104,256]{1,0:T(8,128)(2,1)}, u32[]{:S(2)}) copy-start(bf16[3104,256]{1,0:T(8,128)(2,1)} %constant.16.tables) | copy-start | bytes 4767748
  3.4 25.8 %copy-start.6 = (bf16[32,32]{1,0:T(8,128)(2,1)S(1)}, bf16[32,32]{1,0:T(8,128)(2,1)}, u32[]{:S(2)}) copy-start(bf16[32,32]{1,0:T(8,128)(2,1)} %mixer.1) | copy-start | bytes 6148
  3.4 25.8 %copy-start.7 = (f32[32]{0:T(128)S(1)}, f32[32]{0:T(128)}, u32[]{:S(2)}) copy-start(f32[32]{0:T(128)} %param.12) | copy-start | bytes 388
  29.2 38.0 %copy-start.5 = (bf16[768,256]{1,0:T(8,128)(2,1)S(1)}, bf16[768,256]{1,0:T(8,128)(2,1)}, u32[]{:S(2)}) copy-start(bf16[768,256]{1,0:T(8,128)(2,1)} %constant.17.tables) | copy-start | bytes 1179652
  67.2 6.4 %copy-start.1 = (bf16[32,256,128]{2,1,0:T(8,128)(2,1)S(1)}, bf16[32,256,128]{2,1,0:T(8,128)(2,1)}, u32[]{:S(2)}) copy-start(bf16[32,256,128]{2,1,0:T(8,128)(2,1)} %get-tuple-element.21.mixed_grad) | copy-start | bytes 6291460
  67.2 6.4 %copy-start.4 = (bf16[768,256]{1,0:T(8,128)(2,1)S(1)}, bf16[768,256]{1,0:T(8,128)(2,1)}, u32[]{:S(2)}) copy-start(bf16[768,256]{1,0:T(8,128)(2,1)} %constant.18.tables) | copy-start | bytes 1179652
  73.5 5.9 %copy-start.8 = (bf16[32,256,128]{2,1,0:T(8,128)(2,1)S(1)}, bf16[32,256,128]{2,1,0:T(8,128)(2,1)}, u32[]{:S(2)}) copy-start(bf16[32,256,128]{2,1,0:T(8,128)(2,1)} %get-tuple-element.15) | copy-start | bytes 6291460

commit v4 on v3

--- a/solution.py
+++ b/solution.py
@@ -206,16 +206,26 @@
     return [product[:, half * depth : (half + 1) * depth].reshape(C, band, depth) for half in range(2)]
 
 
-def activate(band, field, upstream, table, offset, spectral, layer_out, slope):
-    alpha = math.sqrt(2.0 / math.pi)
-    cubic = alpha * 0.044715
-
+def mix_state(band, field, table, offset, spectral):
     def bands(step, carry):
         begin = pl.multiple_of(step * 2 * band, 2 * band)
         linear = mixed_field(table, field, begin, band)
         for half in range(2):
+            spectral[:, pl.ds(begin + half * band, band), :] = linear[half] + offset
+        return carry
+
+    lax.fori_loop(0, field.shape[1] // (2 * band), bands, 0)
+
+
+def activate(band, upstream, spectral, layer_out, slope):
+    alpha = math.sqrt(2.0 / math.pi)
+    cubic = alpha * 0.044715
+
+    def bands(step, carry):
+        begin = pl.multiple_of(step * 2 * band, 2 * band)
+        for half in range(2):
             where = pl.ds(begin + half * band, band)
-            v = spectral[:, where, :] + (linear[half] + offset)
+            v = spectral[:, where, :]
             square = v * v
             t = jnp.tanh(v * (alpha + cubic * square))
             gate = 0.5 + 0.5 * t
@@ -225,7 +235,7 @@
             slope[:, where, :] = grad.astype(BF16)
         return carry
 
-    lax.fori_loop(0, field.shape[1] // (2 * band), bands, 0)
+    lax.fori_loop(0, upstream.shape[1] // (2 * band), bands, 0)
 
 
 def mix_gradient(band, slope, table, mixed_grad):
@@ -410,7 +420,7 @@
 def grad_pairs(pack, tables, cells_x, group, pairs, first, weights, loose, gathered, factors):
     rows = 2 * MX
     modes = to_modes(
-        loose, pack.get(tables, "x"), pack.get(tables, "sources"), first, group, pairs, cells_x
+        loose, pack.get(tables, "dual_x"), pack.get(tables, "sources"), first, group, pairs, cells_x
     )
     straight = per_pair(modes, group, 0, rows)
     turned = per_pair(modes, group, rows, 2 * rows)
@@ -424,26 +434,39 @@
     coeff = jnp.concatenate(coeffs, axis=0).astype(BF16) * mask
     spread = mm(coeff, pack.get(tables, "shrink")).astype(BF16)
     from_modes(
-        spread, pack.get(tables, "x_back"), pack.get(tables, "modes"), gathered, first, group,
+        spread, pack.get(tables, "dual_x_back"), pack.get(tables, "modes"), gathered, first, group,
         pairs, cells_x,
     )
     for n in range(group):
         factors[first + n] = stacked[n * rows : (n + 1) * rows]
 
 
-def first_kernel(
-    pack, cells_x, wide, group, field, weights_hbm, tables, own, other, spectrum_t, held, turned,
-    loose, gathered, weights, message, arrived, message_back, mate_out, mate_in, load_sem, *sems,
+def layer_kernel(
+    pack, cells_x, wide, group, band, field, upstream, weights_hbm, mixer, bias, tables, layer_out,
+    mixed_grad, own, other, factors, spectrum_t, held, turned, loose, gathered, weights, load_sem,
+    spectral, slope, own_state, other_state, *rest,
 ):
     me = lax.axis_index("narrow")
-    pairs = message.shape[2]
+    buffers, sems = rest[:10], rest[10:]
+    pairs = own.shape[2]
     greet(wide)
     load = pltpu.make_async_copy(weights_hbm, weights, load_sem)
     load.start()
     y_table, z_table = pack.get(tables, "y", me), pack.get(tables, "z", me)
     forward_transform(lambda c: field[c], y_table, z_table, held, turned, cells_x)
     met(wide)
-    gather_modes(turned, message, arrived, mate_out, mate_in, sems[0:2], sems[2:4], wide)
+
+    def mix_ahead():
+        table = tall_mixer(pack.get(tables, "spread"), mixer[...], band, True)
+        rows = lax.broadcasted_iota(jnp.int32, (C, C), 0)
+        unit = rows == lax.broadcasted_iota(jnp.int32, (C, C), 1)
+        offset = jnp.sum(jnp.where(unit, bias[...], 0.0), axis=1, keepdims=True)[:, :, None]
+        mix_state(band, field, table, offset, spectral)
+
+    message, arrived, back, mate_out, mate_in = buffers[:5]
+    gather_modes(
+        turned, message, arrived, mate_out, mate_in, sems[0:2], sems[2:4], wide, mix_ahead
+    )
     unpack_pairs(arrived, loose)
     load.wait()
 
@@ -454,51 +477,35 @@
         return carry
 
     lax.fori_loop(0, pairs // group, groups, 0)
-    scatter_cells(gathered, message_back, own, other, sems[4:6], sems[6:8], wide)
-
-
-def second_kernel(
-    pack, cells_x, wide, group, band, own_in, other_in, field, upstream, weights_hbm, mixer, bias,
-    tables, layer_out, mixed_grad, own, other, factors, held, turned, loose, gathered, weights, message,
-    arrived, message_back, mate_out, mate_in, load_sem, spectral, slope, *sems,
-):
-    me = lax.axis_index("narrow")
-    pairs = message.shape[2]
-    greet(wide)
-    load = pltpu.make_async_copy(weights_hbm, weights, load_sem)
-    load.start()
+    scatter_cells(gathered, back, own_state, other_state, sems[4:6], sems[6:8], wide)
 
     def put(c, rows):
-        spectral[c] = rows
+        spectral[c] = spectral[c] + rows
 
     y_table, z_table = pack.get(tables, "y_back", me), pack.get(tables, "z_back", me)
-    inverse_transform((own_in, other_in), y_table, z_table, put, held, turned, cells_x)
-    table = tall_mixer(pack.get(tables, "spread"), mixer[...], band, True)
-    unit = lax.broadcasted_iota(jnp.int32, (C, C), 0) == lax.broadcasted_iota(jnp.int32, (C, C), 1)
-    offset = jnp.sum(jnp.where(unit, bias[...], 0.0), axis=1, keepdims=True)[:, :, None]
-    activate(band, field, upstream, table, offset, spectral, layer_out, slope)
-    y_table, z_table = pack.get(tables, "y", me), pack.get(tables, "z", me)
+    inverse_transform((own_state, other_state), y_table, z_table, put, held, turned, cells_x)
+    activate(band, upstream, spectral, layer_out, slope)
+    y_table, z_table = pack.get(tables, "dual_y", me), pack.get(tables, "dual_z", me)
     forward_transform(lambda c: slope[c], y_table, z_table, held, turned, cells_x)
-    met(wide)
-
-    def meanwhile():
-        back = tall_mixer(pack.get(tables, "spread"), mixer[...], band, False)
-        mix_gradient(band, slope, back, mixed_grad)
-
+
+    def mix_back():
+        table = tall_mixer(pack.get(tables, "spread"), mixer[...], band, False)
+        mix_gradient(band, slope, table, mixed_grad)
+
+    message, arrived, back, mate_out, mate_in = buffers[5:]
     gather_modes(
-        turned, message, arrived, mate_out, mate_in, sems[0:2], sems[2:4], wide, meanwhile
+        turned, message, arrived, mate_out, mate_in, sems[8:10], sems[10:12], wide, mix_back
     )
     unpack_pairs(arrived, loose)
-    load.wait()
-
-    def groups(step, carry):
+
+    def grad_groups(step, carry):
         grad_pairs(
             pack, tables, cells_x, group, pairs, step * group, weights, loose, gathered, factors
         )
         return carry
 
-    lax.fori_loop(0, pairs // group, groups, 0)
-    scatter_cells(gathered, message_back, own, other, sems[4:6], sems[6:8], wide)
+    lax.fori_loop(0, pairs // group, grad_groups, 0)
+    scatter_cells(gathered, back, own, other, sems[12:14], sems[14:16], wide)
 
 
 def weight_kernel(pack, group, spectrum_t, factors, tables, weight_grad):
@@ -577,63 +584,45 @@
     local = pl.BlockSpec(memory_space=pltpu.VMEM)
     far = pl.BlockSpec(memory_space=pl.ANY)
     mate = pltpu.VMEM((2, MZ // 2 * MY, lanes), BF16)
+    block = pltpu.VMEM(shape, BF16)
+    buffers = [block, block, block, mate, mate]
+    sems = [pltpu.SemaphoreType.DMA((count,)) for count in (wide, wide, 1, 1) + (wide,) * 4]
     work = [
         held,
         turned,
         pltpu.VMEM((wide * 2 * pairs, lanes), F32),
         pltpu.VMEM((2 * wide * pairs, lanes), F32),
         pltpu.VMEM(weights.shape, BF16),
-        pltpu.VMEM(shape, BF16),
-        pltpu.VMEM(shape, BF16),
-        pltpu.VMEM(shape, BF16),
-        mate,
-        mate,
         pltpu.SemaphoreType.DMA,
+        spectral,
+        pltpu.VMEM((C, flat, depth), BF16),
+        block,
+        block,
     ]
-    sems = [pltpu.SemaphoreType.DMA((count,)) for count in (wide, wide, 1, 1) + (wide,) * 4]
 
     pack = Pack()
-    pack.add("y", y_fwd)
-    pack.add("z", z_fwd)
     for name, table in (
-        ("x", x_fwd), ("x_back", x_inv), ("sources", source_rows), ("modes", mode_rows),
+        ("y", y_fwd), ("z", z_fwd), ("y_back", y_inv), ("z_back", z_inv), ("dual_y", y_dual_inv),
+        ("dual_z", z_inv_back), ("x", x_fwd), ("x_back", x_inv), ("dual_x", x_dual_inv),
+        ("dual_x_back", x_dual_fwd), ("sources", source_rows), ("modes", mode_rows),
         ("copies", copies), ("octets", octets), ("picks", picks), ("doubled", doubled),
+        ("sides", sides), ("shrink", shrink), ("spread", spread),
     ):
         pack.add(name, table)
-    own, other, spectrum_t = pl.pallas_call(
-        functools.partial(first_kernel, pack, cells_x, wide, group),
-        in_specs=[local, far, local],
-        out_specs=[local] * 3,
-        out_shape=[message, message, jax.ShapeDtypeStruct((pairs, C, 2 * MX), BF16)],
-        scratch_shapes=work + sems,
+    layer_out, mixed_grad, own, other, factors, spectrum_t = pl.pallas_call(
+        functools.partial(layer_kernel, pack, cells_x, wide, group, band),
+        in_specs=[local] * 2 + [far] + [local] * 3,
+        out_specs=[local] * 6,
+        out_shape=[
+            field_shape, field_shape, message, message,
+            jax.ShapeDtypeStruct((pairs, 2 * MX, 2 * C), BF16),
+            jax.ShapeDtypeStruct((pairs, C, 2 * MX), BF16),
+        ],
+        scratch_shapes=work + buffers * 2 + sems * 2,
         compiler_params=pltpu.CompilerParams(
             vmem_limit_bytes=VMEM_LIMIT, collective_id=0, has_side_effects=True
         ),
-    )(field, weights, pack.array())
-
-    pack = Pack()
-    pack.add("y", y_dual_inv)
-    pack.add("z", z_inv_back)
-    pack.add("y_back", y_inv)
-    pack.add("z_back", z_inv)
-    for name, table in (
-        ("x", x_dual_inv), ("x_back", x_dual_fwd), ("sources", source_rows), ("modes", mode_rows),
-        ("sides", sides), ("octets", octets), ("shrink", shrink), ("spread", spread),
-    ):
-        pack.add(name, table)
-    layer_out, mixed_grad, own, other, factors = pl.pallas_call(
-        functools.partial(second_kernel, pack, cells_x, wide, group, band),
-        in_specs=[local] * 4 + [far] + [local] * 3,
-        out_specs=[local] * 5,
-        out_shape=[
-            field_shape, field_shape, message, message,
-            jax.ShapeDtypeStruct((pairs, 2 * MX, 2 * C), BF16),
-        ],
-        scratch_shapes=work + [spectral, pltpu.VMEM((C, flat, depth), BF16)] + sems,
-        compiler_params=pltpu.CompilerParams(
-            vmem_limit_bytes=VMEM_LIMIT, collective_id=1, has_side_effects=True
-        ),
-    )(own, other, field, upstream, weights, channel_mixer, channel_bias[None, :], pack.array())
+    )(field, upstream, weights, channel_mixer, channel_bias[None, :], pack.array())
 
     pack = Pack()
     pack.add("octets_t", octets_t)

time: 80.9 us -> 76.9 us (0.951)
  Pallas kernels: 76 us -> 73.3 us
  local copies, waits for them, and re-layouts: 4.06 us -> 2.68 us
    pallas_call x2 -> x1, Pallas kernels: 63.8 us -> 61.1 us  [body(): pl.pallas_call(functools.partial(layer_kernel, pack, cells_x, wide, group...]
    unnamed x19 -> x11, local copies, waits for them, and re-layouts: 4.06 us -> 2.68 us
where the time goes in v4:
time: 76.9 us; the launch traced here: 76.7 us
  Pallas kernels  73.3 us (95%)
  local copies, waits for them, and re-layouts  2.68 us (3%)
    pallas_call x1, Pallas kernels, body(): pl.pallas_call(functools.partial(layer_kernel, pack, cells_x, wide, group...  61.1 us
    pallas_call x1, Pallas kernels, body(): pl.pallas_call(functools.partial(weight_kernel, pack, strip), grid=(pairs...  6.35 us
    pallas_call x1, Pallas kernels, body(): pl.pallas_call(functools.partial(final_kernel, pack, cells_x), out_shape=...  5.86 us
    unnamed x11, local copies, waits for them, and re-layouts  2.68 us

profile of v4, /device:TPU:0, one launch (start us, length us, event | category | flops | bytes accessed | tf_op | source)
XLA Modules:
  0.0 76.7 jit_solution(2142589937005214038)
XLA Ops:
  0.6 0.0 copy-start.3
  0.6 0.7 copy-done.3
  1.3 0.0 copy-start.4
  1.3 0.7 copy-done.4
  2.0 0.0 copy-start.2
  2.0 61.1 %shard_map.103 = (bf16[32,256,128]{2,1,0:T(8,128)(2,1)S(1)}, bf16[32,256,128]{2,1,0:T(8,128)(2,1)}, bf16[8,2,36,128]{3,2,1,0:T(8,128)(2,1)S(1)}, bf16[8,2,36,128...) custom-call(bf16[32,256,128]{2,1,0:T(8,128)(2,1)} %bitcast.12, ...), custom_call_target="tpu_custom_call" | custom-call | tf_op jit(solution)/shard_map/pallas_call | solution.py:612
  63.1 0.0 copy-done.2
  63.1 0.0 copy-start
  63.2 0.0 copy-start.1
  63.2 6.3 %shard_map.104 = f32[27648,64]{1,0:T(8,128)} custom-call(bf16[36,32,48]{2,1,0:T(8,128)(2,1)S(1)} %get-tuple-element.13.spectrum_t, bf16[36,48,64]{2,1,0:T(8,128)(2,1)S(1)} %get-tuple-element.14.factors, bf16[768,256]{1,0:T(8,128)(2,1)S(1)} %copy-done.2), custom_call_target="tpu_custom_call" | custom-call | tf_op jit(solution)/shard_map/pallas_call | solution.py:630
  69.5 0.0 copy-done
  69.5 0.0 copy-done.1
  69.5 5.9 %shard_map.105 = bf16[32,256,128]{2,1,0:T(8,128)(2,1)} custom-call(bf16[8,2,36,128]{3,2,1,0:T(8,128)(2,1)S(1)} %get-tuple-element.15.own, bf16[8,2,36,128]{3,2,1,0:T(8,128)(2,1)S(1)} %get-tuple-element.16.other, bf16[32,256,128]{2,1,0:T(8,128)(2,1)S(1)} %copy-done, bf16[768,256]{1,0:T(8,128)(2,1)S(1)} %copy-done.1), custom_call_target="tpu_custom_call" | custom-call | tf_op jit(solution)/shard_map/pallas_call | solution.py:647
  75.4 1.3 %copy.12 = bf16[32,4,64,128]{3,2,1,0:T(8,128)(2,1)} copy(bf16[32,4,64,128]{3,2,1,0:T(8,128)(2,1)S(1)} %bitcast.7) | data formatting | bytes 4194304
Async XLA Ops:
  0.6 0.7 copy-start.3
  1.3 0.7 copy-start.4
  2.0 61.2 %copy-start.2 = (bf16[768,256]{1,0:T(8,128)(2,1)S(1)}, bf16[768,256]{1,0:T(8,128)(2,1)}, u32[]{:S(2)}) copy-start(bf16[768,256]{1,0:T(8,128)(2,1)} %constant.13.tables) | copy-start | bytes 1179652
  63.1 6.4 %copy-start = (bf16[32,256,128]{2,1,0:T(8,128)(2,1)S(1)}, bf16[32,256,128]{2,1,0:T(8,128)(2,1)}, u32[]{:S(2)}) copy-start(bf16[32,256,128]{2,1,0:T(8,128)(2,1)} %get-tuple-element.17.mixed_grad) | copy-start | bytes 6291460
  63.2 6.4 %copy-start.1 = (bf16[768,256]{1,0:T(8,128)(2,1)S(1)}, bf16[768,256]{1,0:T(8,128)(2,1)}, u32[]{:S(2)}) copy-start(bf16[768,256]{1,0:T(8,128)(2,1)} %constant.14.tables) | copy-start | bytes 1179652
